TPU v7x, 32 devices: a whole 2x2x4 slice. The times are simulated.
32 devices in a mesh: gx: 8 (over y, x, core), gy: 4 (over z).
Axes of the slice: x: 2, y: 2, z: 4, core: 2. Of those that a mesh axis runs over, the one named last changes fastest.
Arguments:
- factor: bfloat16 [64, 64, 64, 256], P(None, 'gx', 'gy'), may hold values from -200 to 200
- offset: int32 [1], replicated, may hold values from 0 to 32
- diagonal: float32 [64, 64, 256], P('gx', 'gy'), may hold values from 0.25 to 16
- actuators: bfloat16 [8, 64, 64, 256], P(None, 'gx', 'gy'), may hold values from -200 to 200
- sensors: bfloat16 [8, 64, 64, 256], P(None, 'gx', 'gy'), may hold values from -200 to 200
Outputs:
- rotated: bfloat16 [32, 64, 64, 256], P(None, 'gx', 'gy')
- residual_factor: bfloat16 [32, 64, 64, 256], P(None, 'gx', 'gy')
- riccati: float32 [32, 32], replicated
- gram_first: float32 [32, 32], replicated
All inputs are finite; a program needn't handle non-finite values.
Results may differ from a plain program's by a relative error of at most 0.0034.
Values may be sent and summed in bfloat16 or wider, within the bound.
No kernel may reach another device: no remote copies, remote signals or barrier semaphores. Data moves between devices by JAX's collectives and lax.ppermute only.
A program may use at most 128 MiB of HBM per device.

v0:
```python
import functools
import math

import jax
import jax.numpy as jnp
from jax import lax
from jax.experimental import pallas as pl
from jax.experimental.pallas import tpu as pltpu
from jax.sharding import PartitionSpec as P

WINDOW = 32
KLEIN = 3
SMITH = 4
SUB = 8
ROWS = WINDOW * SUB
PANEL = 8
GROUP = 8
SHIFT = 2.0**-15
FLOOR = 1e-30

f32 = jnp.float32
bf16 = jnp.bfloat16
highest = lax.Precision.HIGHEST
NT = (((1,), (1,)), ((), ()))
NN = (((1,), (0,)), ((), ()))


def mm(left, right, dims=NN):
    return lax.dot_general(left, right, dims, precision=highest, preferred_element_type=f32)


def dot(left, right, dims=NN):
    return lax.dot_general(left, right, dims, preferred_element_type=f32)


def split(value):
    high = value.astype(bf16)
    return high, (value - high.astype(f32)).astype(bf16)


def split_three(value):
    high = value.astype(bf16)
    rest = value - high.astype(f32)
    middle = rest.astype(bf16)
    return high, middle, (rest - middle.astype(f32)).astype(bf16)


def iota(shape, dim):
    return lax.broadcasted_iota(jnp.int32, shape, dim)


def eye(size):
    return (iota((size, size), 0) == iota((size, size), 1)).astype(f32)


def diagonal_of(matrix):
    size = matrix.shape[0]
    mask = iota((size, size), 0) == iota((size, size), 1)
    return jnp.sum(jnp.where(mask, matrix, 0.0), axis=1, keepdims=True)


def eliminate(matrix, full):
    size, width = matrix.shape
    row = iota((size, width), 0)
    for start in range(0, size, PANEL):
        columns = [
            jnp.broadcast_to(matrix[:, start + t : start + t + 1], (size, width)) for t in range(PANEL)
        ]
        for t in range(PANEL):
            at = start + t
            factor = columns[t] * (1.0 / columns[t][at : at + 1, :])
            factor = jnp.where(row != at if full else row > at, factor, 0.0)
            for s in range(t + 1, PANEL):
                columns[s] = columns[s] - factor * columns[s][at : at + 1, :]
            matrix = matrix - factor * matrix[at : at + 1, :]
    return matrix


def cholesky_inverse(gram):
    size = gram.shape[0]
    matrix = eliminate(jnp.concatenate([gram, eye(size)], axis=1), False)
    upper = matrix[:, :size]
    scale = lax.rsqrt(diagonal_of(upper))
    upper = jnp.where(iota((size, size), 0) <= iota((size, size), 1), upper, 0.0)
    return upper * scale, matrix[:, size:] * scale


def solve(square, right):
    size = square.shape[0]
    matrix = eliminate(jnp.concatenate([square, right], axis=1), True)
    return matrix[:, size:] / diagonal_of(matrix[:, :size])


def spread_matrix(count):
    return ((iota((count * SUB, count), 0) >> 3) == iota((count * SUB, count), 1)).astype(bf16)


def same_row(rows, columns):
    return (iota((rows, columns), 0) & 7) == (iota((rows, columns), 1) & 7)


def expand(pieces):
    spread = spread_matrix(WINDOW)
    mask = same_row(ROWS, ROWS)
    out = []
    for piece in pieces:
        tall = dot(spread, piece).astype(bf16)
        out.append(jnp.where(mask, dot(tall, spread, NT), 0.0).astype(bf16))
    return out


def reduce_rows(total):
    rows, columns = total.shape
    count = columns // SUB
    kept = jnp.where(same_row(rows, columns), total, 0.0)
    kept = jnp.sum(kept.reshape(rows // SUB, SUB, columns), axis=1)
    return mm(kept, spread_matrix(count).astype(f32))


def block(rows, half):
    part = rows[:, half * SUB : (half + 1) * SUB]
    return part.reshape(rows.shape[0] * SUB, rows.shape[2]).astype(bf16)


def window_copies(scalars, factor, window, sems):
    planes = window.shape[1]
    return [
        pltpu.make_async_copy(
            factor.at[pl.ds(scalars[0], WINDOW), pl.ds(x, 1)], window.at[:, pl.ds(x, 1)], sems.at[x]
        )
        for x in range(planes)
    ]


def frame_kernel(weight, scalars, factor, small, x_even, x_odd, y_even, y_odd, window, total, sems):
    planes, rows, depth = window.shape[1:]
    copies = window_copies(scalars, factor, window, sems)
    for copy in copies:
        copy.start()
    sub = iota((WINDOW, planes, depth), 1)
    low_y = jnp.zeros((WINDOW, planes, depth), f32)
    high_y = jnp.zeros((WINDOW, planes, depth), f32)
    for x in range(planes):
        copies[x].wait()
        plane = window[:, x].astype(f32)
        products = None
        for half in range(rows // SUB):
            rows_here = block(plane, half)
            product = dot(rows_here, rows_here, NT)
            products = product if products is None else products + product
        if x == 0:
            total[...] = products
        else:
            total[...] += products
        low_y = jnp.where(sub == x, jnp.broadcast_to(plane[:, :1], low_y.shape), low_y)
        high_y = jnp.where(sub == x, jnp.broadcast_to(plane[:, rows - 1 :], high_y.shape), high_y)
    x_first = scalars[1] == 0
    y_first = scalars[2] == 0
    first, last = window[:, 0], window[:, planes - 1]
    x_even[...] = jnp.where(x_first, last, first)
    x_odd[...] = jnp.where(x_first, first, last)
    low_y = low_y.reshape(WINDOW * planes, depth).astype(bf16)
    high_y = high_y.reshape(WINDOW * planes, depth).astype(bf16)
    y_even[...] = jnp.where(y_first, high_y, low_y)
    y_odd[...] = jnp.where(y_first, low_y, high_y)
    gram = reduce_rows(total[...]) * weight
    on = eye(WINDOW)
    upper, inverse = cholesky_inverse(gram + on * (SHIFT * gram + FLOOR))
    lower_gram = jnp.where(iota(gram.shape, 0) > iota(gram.shape, 1), gram, 0.0)
    small[...] = jnp.concatenate(
        [upper + lower_gram, inverse, diagonal_of(gram), jnp.zeros((WINDOW, 63), f32)], axis=1
    )


def project_kernel(
    weight, scalars, small, factor, x_even, x_odd, y_even, y_odd, diagonal, actuators, sensors,
    payload, fields, window, rows_all, low_y, high_y, held, gram_a, gram_b, image_a, input_a, sems, out_sems,
):
    planes, rows, depth = window.shape[1:]
    halves = rows // SUB
    copies = window_copies(scalars, factor, window, sems)
    for copy in copies:
        copy.start()
    frame = expand(split_three(small[:, WINDOW : 2 * WINDOW]))

    def transform(rows_here):
        return dot(frame[0], rows_here) + dot(frame[1], rows_here) + dot(frame[2], rows_here)

    x_first = scalars[1] == 0
    y_first = scalars[2] == 0
    even, odd = x_even[...].astype(f32), x_odd[...].astype(f32)
    low, high = jnp.where(x_first, odd, even), jnp.where(x_first, even, odd)
    for half in range(halves):
        rows_all[0, half] = transform(block(low, half))
        rows_all[planes + 1, half] = transform(block(high, half))
    even, odd = y_even[...].astype(f32), y_odd[...].astype(f32)
    low_y[...] = transform(jnp.where(y_first, odd, even).astype(bf16))
    high_y[...] = transform(jnp.where(y_first, even, odd).astype(bf16))
    for copy in copies:
        copy.wait()

    def transform_plane(x, carry):
        plane = window[:, x].astype(f32)
        for half in range(halves):
            rows_all[x + 1, half] = transform(block(plane, half))
        return carry

    lax.fori_loop(0, planes, transform_plane, 0)
    gram_a[...] = jnp.zeros_like(gram_a)
    gram_b[...] = jnp.zeros_like(gram_b)
    image_a[...] = jnp.zeros_like(image_a)
    input_a[...] = jnp.zeros_like(input_a)
    tile = (WINDOW, SUB, depth)

    def out_copy(x):
        return pltpu.make_async_copy(held.at[x], fields.at[x], out_sems.at[x])

    def plane_step(x, carry):
        sub = iota(tile, 1)
        lane = iota(tile, 2)
        here = [rows_all[x + 1, half].reshape(tile) for half in range(halves)]
        up = [pltpu.roll(value, 1, 1) for value in here]
        down = [pltpu.roll(value, SUB - 1, 1) for value in here]
        before = pltpu.roll(low_y[...].reshape(tile), lax.rem(SUB - x, SUB), 1)
        after = pltpu.roll(high_y[...].reshape(tile), lax.rem(2 * SUB - 1 - x, SUB), 1)
        act_plane, sens_plane = actuators[:, x].astype(f32), sensors[:, x].astype(f32)
        for half in range(halves):
            value = here[half]
            above = jnp.where(sub == 0, before if half == 0 else up[half - 1], up[half])
            below = jnp.where(sub == SUB - 1, after if half == halves - 1 else down[half + 1], down[half])
            beside = rows_all[x, half].reshape(tile) + rows_all[x + 2, half].reshape(tile)
            beside = beside + above + below
            beside = beside + jnp.where(lane == depth - 1, 0.0, pltpu.roll(value, depth - 1, 2))
            beside = beside + jnp.where(lane == 0, 0.0, pltpu.roll(value, 1, 2))
            coefficient = 6.0 + diagonal[x, half * SUB : (half + 1) * SUB, :]
            image = (beside - coefficient[None] * value).reshape(ROWS, depth)
            field_high, field_low = split(value.reshape(ROWS, depth))
            image_high, image_low = split(image)
            held[x, half, 0] = field_high
            held[x, half, 1] = field_low
            held[x, half, 2] = image_high
            held[x, half, 3] = image_low
            gram_a[...] += dot(field_high, field_high, NT)
            gram_b[...] += dot(field_high, field_low, NT)
            image_a[...] += (
                dot(field_high, image_high, NT) + dot(field_low, image_high, NT) + dot(field_high, image_low, NT)
            )
            inputs = jnp.concatenate([block(act_plane, half), block(sens_plane, half)], axis=0)
            input_a[...] += dot(field_high, inputs, NT) + dot(field_low, inputs, NT)
        out_copy(x).start()
        return carry

    lax.fori_loop(0, planes, plane_step, 0)
    cross = reduce_rows(gram_b[...])
    gram = (reduce_rows(gram_a[...]) + cross + cross.T) * weight
    image_gram = reduce_rows(image_a[...]) * weight
    inputs = reduce_rows(input_a[...]) * weight
    packed = jnp.concatenate(
        [small[:, :WINDOW], gram, image_gram, inputs, small[:, 2 * WINDOW : 2 * WINDOW + 1],
         jnp.zeros((WINDOW, 15), f32)], axis=1,
    )
    payload[...] = jnp.broadcast_to(packed[None], payload.shape)
    for x in range(planes):
        out_copy(x).wait()


def lyapunov_factor(start, cayley):
    for doubling in range(SMITH):
        start = jnp.concatenate([start, mm(cayley, start)], axis=1)
        if doubling < SMITH - 1:
            cayley = mm(cayley, cayley)
    return mm(start, start, NT)


def riccati_solve(resolvent, drive, sense):
    inputs = drive.shape[1]
    on = eye(WINDOW)
    on_small = eye(inputs)
    root = math.sqrt(2.0)
    sense_row = mm(resolvent, sense)
    drive_row = mm(resolvent, drive)
    riccati = lyapunov_factor(root * sense_row, on - 2.0 * resolvent)
    for _ in range(KLEIN - 1):
        state = mm(riccati, drive)
        moved = mm(resolvent, state)
        small = on_small + mm(drive.T, moved)
        inverse = solve(mm(small.T, small), small.T)
        scaled = mm(moved, inverse)
        shifted = resolvent - mm(scaled, drive_row, NT)
        start = jnp.concatenate([sense_row - mm(scaled, mm(drive_row.T, sense)), scaled], axis=1)
        riccati = lyapunov_factor(root * start, on - 2.0 * shifted)
    return riccati


def finish_kernel(
    small, gathered, fields, rotated, residual, riccati_out, gram_out,
    held, rotated_held, residual_held, sems, out_sems,
):
    planes, halves = held.shape[:2]
    devices = gathered.shape[0]
    copies = [pltpu.make_async_copy(fields.at[x], held.at[x], sems.at[x]) for x in range(planes)]
    for copy in copies:
        copy.start()
    row, column = iota((WINDOW, WINDOW), 0), iota((WINDOW, WINDOW), 1)
    triangle = row <= column
    summed = jnp.sum(gathered[...], axis=0)
    lower = jnp.where(row > column, summed[:, :WINDOW], 0.0)
    gram = lower + lower.T + jnp.where(row == column, summed[:, 112:113], 0.0)
    gram_out[...] = gram
    _, first = cholesky_inverse(gram)

    wide = GROUP * WINDOW
    repeat = ((iota((WINDOW, wide), 1) & (WINDOW - 1)) == iota((WINDOW, wide), 0)).astype(bf16)
    same_block = (iota((wide, wide), 0) // WINDOW) == (iota((wide, wide), 1) // WINDOW)
    stack_triangle = (iota((wide, WINDOW), 0) & (WINDOW - 1)) <= iota((wide, WINDOW), 1)

    def block_diagonal(stack):
        return jnp.where(same_block, dot(stack, repeat), 0.0).astype(bf16)

    def times(left, pieces):
        left_high, left_low = split(left)
        return dot(left_high, pieces[0]) + dot(left_low, pieces[0]) + dot(left_high, pieces[1])

    def group_step(group, totals):
        stack = gathered[pl.ds(group * GROUP, GROUP)].reshape(wide, gathered.shape[2])
        factors = jnp.where(stack_triangle, stack[:, :WINDOW], 0.0)
        change = mm(first, factors, NT)
        grams = [block_diagonal(piece) for piece in split(stack[:, WINDOW : 2 * WINDOW])]
        images = [block_diagonal(piece) for piece in split(stack[:, 2 * WINDOW : 3 * WINDOW])]
        return (
            totals[0] + mm(times(change, grams), change, NT),
            totals[1] + mm(times(change, images), change, NT),
            totals[2] + mm(change, stack[:, 3 * WINDOW : 3 * WINDOW + 16]),
        )

    totals = (jnp.zeros((WINDOW, WINDOW), f32), jnp.zeros((WINDOW, WINDOW), f32), jnp.zeros((WINDOW, 16), f32))
    groups = devices // GROUP
    if groups <= 4:
        for group in range(groups):
            totals = group_step(group, totals)
    else:
        totals = lax.fori_loop(0, groups, group_step, totals)
    gram_second, raw, inputs = totals
    raw = 0.5 * (raw + raw.T)
    upper, second = cholesky_inverse(gram_second)
    core = solve(gram_second - raw, eye(WINDOW))
    resolvent = mm(mm(upper, core), upper, NT)
    inputs = mm(second, inputs)
    projected = mm(mm(second, raw), second, NT)
    riccati = riccati_solve(resolvent, inputs[:, :8], inputs[:, 8:])
    riccati_out[...] = riccati
    own = jnp.where(triangle, small[:, :WINDOW], 0.0)
    change = mm(mm(second, first), own, NT)
    rotate = mm(riccati, change)
    remove = -mm(riccati, mm(projected, change))
    rotate_high, rotate_low, remove_high, remove_low = expand(split(rotate) + split(remove))
    for copy in copies:
        copy.wait()

    def out_copies(x):
        return (
            pltpu.make_async_copy(rotated_held.at[:, pl.ds(x, 1)], rotated.at[:, pl.ds(x, 1)], out_sems.at[0, x]),
            pltpu.make_async_copy(residual_held.at[:, pl.ds(x, 1)], residual.at[:, pl.ds(x, 1)], out_sems.at[1, x]),
        )

    def plane_step(x, carry):
        turned, left = [], []
        for half in range(halves):
            field_high, field_low = held[x, half, 0], held[x, half, 1]
            image_high, image_low = held[x, half, 2], held[x, half, 3]
            depth = field_high.shape[1]
            here = dot(rotate_high, field_high) + dot(rotate_low, field_high) + dot(rotate_high, field_low)
            rest = dot(rotate_high, image_high) + dot(rotate_low, image_high) + dot(rotate_high, image_low)
            rest = rest + (dot(remove_high, field_high) + dot(remove_low, field_high) + dot(remove_high, field_low))
            turned.append(here.reshape(WINDOW, SUB, depth))
            left.append(rest.reshape(WINDOW, SUB, depth))
        rotated_held[:, x] = jnp.concatenate(turned, axis=1).astype(bf16)
        residual_held[:, x] = jnp.concatenate(left, axis=1).astype(bf16)
        for copy in out_copies(x):
            copy.start()
        return carry

    lax.fori_loop(0, planes, plane_step, 0)
    for x in range(planes):
        for copy in out_copies(x):
            copy.wait()


def exchange(face, axis, odd):
    count = lax.axis_size(axis)
    first = 1 if odd else 0
    pairs = [(i, i + 1) for i in range(first, count - 1, 2)]
    return lax.ppermute(face, axis, pairs + [(b, a) for a, b in pairs])


vmem = pl.BlockSpec(memory_space=pltpu.VMEM)
smem = pl.BlockSpec(memory_space=pltpu.SMEM)
anywhere = pl.BlockSpec(memory_space=pl.ANY)


def params(megabytes):
    return pltpu.CompilerParams(vmem_limit_bytes=megabytes * 2**20)


def local(factor, offset, diagonal, actuators, sensors):
    planes, rows, depth = factor.shape[1:]
    devices = lax.axis_size("gx") * lax.axis_size("gy")
    weight = 1.0 / (planes * rows * depth * devices)
    shape = jax.ShapeDtypeStruct
    window_shape = (WINDOW, planes, rows, depth)
    halves = rows // SUB
    scalars = jnp.stack([offset[0], lax.axis_index("gx") % 2, lax.axis_index("gy") % 2]).astype(jnp.int32)
    x_face = shape((WINDOW, rows, depth), bf16)
    y_face = shape((WINDOW * planes, depth), bf16)
    small, x_even, x_odd, y_even, y_odd = pl.pallas_call(
        functools.partial(frame_kernel, weight),
        out_shape=(shape((WINDOW, 128), f32), x_face, x_face, y_face, y_face),
        in_specs=[smem, anywhere],
        out_specs=(vmem,) * 5,
        scratch_shapes=[
            pltpu.VMEM(window_shape, bf16),
            pltpu.VMEM((ROWS, ROWS), f32),
            pltpu.SemaphoreType.DMA((planes,)),
        ],
        compiler_params=params(24),
        name="frame",
    )(scalars, factor)
    x_even = exchange(x_even, "gx", False)
    x_odd = exchange(x_odd, "gx", True)
    y_even = exchange(y_even, "gy", False)
    y_odd = exchange(y_odd, "gy", True)
    fields_shape = (planes, halves, 4, ROWS, depth)
    payload, fields = pl.pallas_call(
        functools.partial(project_kernel, weight),
        out_shape=(shape((devices, WINDOW, 128), f32), shape(fields_shape, bf16)),
        in_specs=[smem, vmem, anywhere] + [vmem] * 7,
        out_specs=(vmem, anywhere),
        scratch_shapes=[
            pltpu.VMEM(window_shape, bf16),
            pltpu.VMEM((planes + 2, halves, ROWS, depth), f32),
            pltpu.VMEM((WINDOW * planes, depth), f32),
            pltpu.VMEM((WINDOW * planes, depth), f32),
            pltpu.VMEM(fields_shape, bf16),
            pltpu.VMEM((ROWS, ROWS), f32),
            pltpu.VMEM((ROWS, ROWS), f32),
            pltpu.VMEM((ROWS, ROWS), f32),
            pltpu.VMEM((ROWS, 16 * SUB), f32),
            pltpu.SemaphoreType.DMA((planes,)),
            pltpu.SemaphoreType.DMA((planes,)),
        ],
        compiler_params=params(40),
        name="project",
    )(scalars, small, factor, x_even, x_odd, y_even, y_odd, diagonal, actuators, sensors)
    gathered = lax.all_to_all(payload, ("gx", "gy"), 0, 0)
    return pl.pallas_call(
        finish_kernel,
        out_shape=(
            shape(window_shape, bf16),
            shape(window_shape, bf16),
            shape((WINDOW, WINDOW), f32),
            shape((WINDOW, WINDOW), f32),
        ),
        in_specs=[vmem, vmem, anywhere],
        out_specs=(anywhere, anywhere, vmem, vmem),
        scratch_shapes=[
            pltpu.VMEM(fields_shape, bf16),
            pltpu.VMEM(window_shape, bf16),
            pltpu.VMEM(window_shape, bf16),
            pltpu.SemaphoreType.DMA((planes,)),
            pltpu.SemaphoreType.DMA((2, planes)),
        ],
        compiler_params=params(40),
        name="finish",
    )(small, gathered, fields)


def solution(mesh):
    return jax.shard_map(
        local,
        mesh=mesh,
        in_specs=(
            P(None, "gx", "gy", None),
            P(),
            P("gx", "gy", None),
            P(None, "gx", "gy", None),
            P(None, "gx", "gy", None),
        ),
        out_specs=(P(None, "gx", "gy", None), P(None, "gx", "gy", None), P(), P()),
        check_vma=False,
    )
```

profile of v0, /device:TPU:0, one launch (start us, length us, event | category | flops | bytes accessed | tf_op | source)
XLA Modules:
  0.0 79.1 jit_solution(18386156131853287310)
XLA Ops:
  1.3 0.1 pad_add_fusion.scalars
  1.4 0.0 copy-start
  1.4 2.2 %copy-done = bf16[64,8,16,256]{3,2,1,0:T(8,128)(2,1)S(1)} copy-done((bf16[64,8,16,256]{3,2,1,0:T(8,128)(2,1)S(1)}, bf16[64,8,16,256]{3,2,1,0:T(8,128)(2,1)}, u32[]{:S(2)}) %copy-start) | copy-done | bytes 4194328
  3.6 0.0 copy-start.1
  3.6 3.8 %frame.1 = (f32[32,128]{1,0:T(8,128)S(1)}, bf16[32,16,256]{2,1,0:T(8,128)(2,1)S(1)}, bf16[32,16,256]{2,1,0:T(8,128)(2,1)S(1)}, bf16[256,256]{1,0:T(8,128)(2,1)S(1)}, bf16[256,256]{1,0:T(8,128)(2,1)S(1)}) custom-call(s32[3]{0:T(128)S(1)} %pad_add_fusion.scalars, bf16[64,8,16,256]{3,2,1,0:T(8,128)(2,1)S(1)} %copy-done), custom_call_target="tpu_custom_call" | custom-call | tf_op jit(solution)/shard_map/frame/pallas_call | solution.py:415
  7.4 0.5 collective-permute-start
  7.9 0.7 collective-permute-start.1
  8.5 2.7 %collective-permute-start.2 = (bf16[256,256]{1,0:T(8,128)(2,1)S(1)}, bf16[256,256]{1,0:T(8,128)(2,1)S(1)}, u32[]{:S(2)}, u32[]{:S(2)}) collective-permute-start(bf16[256,256]{1,0:T(8,128)(2,1)S(1)} %get-tuple-element.14), channel_id=1, source_target_pairs={{0,1},{2,3},{1,0},{3,2},{4,5},{6,7},{5,4},{7,6},{8,9},{10,11},{9,8... | collective-permute-start | bytes 393224 | tf_op jit(solution)/shard_map/ppermute | solution.py:393
  11.2 0.7 collective-permute-start.3
  11.9 2.3 %collective-permute-done.2.y_even = bf16[256,256]{1,0:T(8,128)(2,1)S(1)} collective-permute-done((bf16[256,256]{1,0:T(8,128)(2,1)S(1)}, bf16[256,256]{1,0:T(8,128)(2,1)S(1)}, u32[]{:S(2)}, u32[]{:S(2)}) %collective-permute-start.2) | collective-permute-done | bytes 131104 | tf_op jit(solution)/shard_map/ppermute | solution.py:393
  14.2 0.0 collective-permute-done.3.y_odd
  14.2 0.0 collective-permute-done.x_even
  14.2 0.0 collective-permute-done.1.x_odd
  14.2 0.0 copy-done.1
  14.2 0.0 copy-start.3
  14.2 1.0 %copy-done.3 = bf16[8,8,16,256]{3,2,1,0:T(8,128)(2,1)S(1)} copy-done((bf16[8,8,16,256]{3,2,1,0:T(8,128)(2,1)S(1)}, bf16[8,8,16,256]{3,2,1,0:T(8,128)(2,1)}, u32[]{:S(2)}) %copy-start.3) | copy-done | bytes 524312
  15.2 0.0 copy-start.4
  15.2 1.0 %copy-done.4 = bf16[8,8,16,256]{3,2,1,0:T(8,128)(2,1)S(1)} copy-done((bf16[8,8,16,256]{3,2,1,0:T(8,128)(2,1)S(1)}, bf16[8,8,16,256]{3,2,1,0:T(8,128)(2,1)}, u32[]{:S(2)}) %copy-start.4) | copy-done | bytes 524312
  16.3 0.0 copy-start.5
  16.3 0.9 %copy-done.5 = f32[8,16,256]{2,1,0:T(8,128)S(1)} copy-done((f32[8,16,256]{2,1,0:T(8,128)S(1)}, f32[8,16,256]{2,1,0:T(8,128)}, u32[]{:S(2)}) %copy-start.5) | copy-done | bytes 131096
  17.2 12.9 %project.1 = (f32[32,32,128]{2,1,0:T(8,128)S(1)}, bf16[8,2,4,256,256]{4,3,2,1,0:T(8,128)(2,1)}) custom-call(s32[3]{0:T(128)S(1)} %pad_add_fusion.scalars, f32[32,128]{1,0:T(8,128)S(1)} %get-tuple-element.11.small, bf16[64,8,16,256]{3,2,1,0:T(8,128)(2,1)S(1)} %copy-done.1, bf16[32,16,256]{2,1,0:T(8,128)(2,1)S(1)} %collective-permute-done.x_even, ...), custom_call_target="tpu_custom_call" | custom-call | tf_op jit(solution)/shard_map/project/pallas_call | solution.py:433
  30.0 25.0 %all_to_all.5.gathered = f32[32,32,128]{2,1,0:T(8,128)S(1)} all-to-all(f32[32,32,128]{2,1,0:T(8,128)S(1)} %get-tuple-element.16), channel_id=1, replica_groups=mesh['gx'=8,'gy'=4] {'gx','gy'}, dimensions={0} | all-to-all | bytes 1048576 | tf_op jit(solution)/shard_map/all_to_all | solution.py:454
  55.0 3.4 %copy-done.2 = bf16[8,2,4,256,256]{4,3,2,1,0:T(8,128)(2,1)S(1)} copy-done((bf16[8,2,4,256,256]{4,3,2,1,0:T(8,128)(2,1)S(1)}, bf16[8,2,4,256,256]{4,3,2,1,0:T(8,128)(2,1)}, u32[]{:S(2)}) %copy-start.2) | copy-done | bytes 8388632
  58.4 20.7 %finish.1 = (bf16[32,8,16,256]{3,2,1,0:T(8,128)(2,1)}, bf16[32,8,16,256]{3,2,1,0:T(8,128)(2,1)}, f32[32,32]{1,0:T(8,128)}, f32[32,32]{1,0:T(8,128)}) custom-call(f32[32,128]{1,0:T(8,128)S(1)} %get-tuple-element.11.small, f32[32,32,128]{2,1,0:T(8,128)S(1)} %all_to_all.5.gathered, bf16[8,2,4,256,256]{4,3,2,1,0:T(8,128)(2,1)S(1)} %copy-done.2), custom_call_target="tpu_custom_call" | custom-call | tf_op jit(solution)/shard_map/finish/pallas_call | solution.py:455
  (1 shorter events, 0.0 us)
Async XLA Ops:
  1.4 2.2 %copy-start = (bf16[64,8,16,256]{3,2,1,0:T(8,128)(2,1)S(1)}, bf16[64,8,16,256]{3,2,1,0:T(8,128)(2,1)}, u32[]{:S(2)}) copy-start(bf16[64,8,16,256]{3,2,1,0:T(8,128)(2,1)} %factor.3) | copy-start | bytes 12582916
  3.6 10.6 %copy-start.1 = (bf16[64,8,16,256]{3,2,1,0:T(8,128)(2,1)S(1)}, bf16[64,8,16,256]{3,2,1,0:T(8,128)(2,1)}, u32[]{:S(2)}) copy-start(bf16[64,8,16,256]{3,2,1,0:T(8,128)(2,1)} %factor.3) | copy-start | bytes 12582916
  7.4 6.8 %collective-permute-start = (bf16[32,16,256]{2,1,0:T(8,128)(2,1)S(1)}, bf16[32,16,256]{2,1,0:T(8,128)(2,1)S(1)}, u32[]{:S(2)}, u32[]{:S(2)}) collective-permute-start(bf16[32,16,256]{2,1,0:T(8,128)(2,1)S(1)} %get-tuple-element.12), channel_id=1, source_target_pairs={{0,4},{8,12},{16,20},{24,28},{4,0},{12,8},{20,16},{28,24},{1,5},{9... | collective-permute-start | bytes 786440 | tf_op jit(solution)/shard_map/ppermute | solution.py:393
  7.9 6.3 %collective-permute-start.1 = (bf16[32,16,256]{2,1,0:T(8,128)(2,1)S(1)}, bf16[32,16,256]{2,1,0:T(8,128)(2,1)S(1)}, u32[]{:S(2)}, u32[]{:S(2)}) collective-permute-start(bf16[32,16,256]{2,1,0:T(8,128)(2,1)S(1)} %get-tuple-element.13), channel_id=1, source_target_pairs={{4,8},{12,16},{20,24},{8,4},{16,12},{24,20},{5,9},{13,17},{21,25},... | collective-permute-start | bytes 786440 | tf_op jit(solution)/shard_map/ppermute | solution.py:393
  8.5 5.6 %collective-permute-start.2 = (bf16[256,256]{1,0:T(8,128)(2,1)S(1)}, bf16[256,256]{1,0:T(8,128)(2,1)S(1)}, u32[]{:S(2)}, u32[]{:S(2)}) collective-permute-start(bf16[256,256]{1,0:T(8,128)(2,1)S(1)} %get-tuple-element.14), channel_id=1, source_target_pairs={{0,1},{2,3},{1,0},{3,2},{4,5},{6,7},{5,4},{7,6},{8,9},{10,11},{9,8... | collective-permute-start | bytes 393224 | tf_op jit(solution)/shard_map/ppermute | solution.py:393
  11.2 3.0 %collective-permute-start.3 = (bf16[256,256]{1,0:T(8,128)(2,1)S(1)}, bf16[256,256]{1,0:T(8,128)(2,1)S(1)}, u32[]{:S(2)}, u32[]{:S(2)}) collective-permute-start(bf16[256,256]{1,0:T(8,128)(2,1)S(1)} %get-tuple-element.15), channel_id=1, source_target_pairs={{1,2},{2,1},{5,6},{6,5},{9,10},{10,9},{13,14},{14,13},{17,18},{18,... | collective-permute-start | bytes 393224 | tf_op jit(solution)/shard_map/ppermute | solution.py:393
  14.2 1.0 %copy-start.3 = (bf16[8,8,16,256]{3,2,1,0:T(8,128)(2,1)S(1)}, bf16[8,8,16,256]{3,2,1,0:T(8,128)(2,1)}, u32[]{:S(2)}) copy-start(bf16[8,8,16,256]{3,2,1,0:T(8,128)(2,1)} %actuators.1) | copy-start | bytes 1572868
  15.2 1.0 %copy-start.4 = (bf16[8,8,16,256]{3,2,1,0:T(8,128)(2,1)S(1)}, bf16[8,8,16,256]{3,2,1,0:T(8,128)(2,1)}, u32[]{:S(2)}) copy-start(bf16[8,8,16,256]{3,2,1,0:T(8,128)(2,1)} %sensors.1) | copy-start | bytes 1572868
  16.3 0.9 %copy-start.5 = (f32[8,16,256]{2,1,0:T(8,128)S(1)}, f32[8,16,256]{2,1,0:T(8,128)}, u32[]{:S(2)}) copy-start(f32[8,16,256]{2,1,0:T(8,128)} %diagonal.1) | copy-start | bytes 393220
  55.0 3.4 %copy-start.2 = (bf16[8,2,4,256,256]{4,3,2,1,0:T(8,128)(2,1)S(1)}, bf16[8,2,4,256,256]{4,3,2,1,0:T(8,128)(2,1)}, u32[]{:S(2)}) copy-start(bf16[8,2,4,256,256]{4,3,2,1,0:T(8,128)(2,1)} %get-tuple-element.17.fields) | copy-start | bytes 25165828
where the time goes:
time: 80.2 us; the launch traced here: 79.1 us
  Pallas kernels  37.3 us (47%)
  blocking collectives  25 us (31%)
  local copies, waits for them, and re-layouts  8.56 us (11%)
  starting transfers between devices  4.51 us (6%)
  waiting for transfers between devices  2.29 us (3%)
  between operations  1.35 us (2%)
    all_to_all x1, blocking collectives, local(): gathered = lax.all_to_all(payload, ('gx', 'gy'), 0, 0)  25 us
    pallas_call x1, Pallas kernels, local(): pl.pallas_call(finish_kernel, out_shape=(shape(window_shape, bf16), shape...  20.7 us
    pallas_call x1, Pallas kernels, local(): pl.pallas_call(functools.partial(project_kernel, weight), out_shape=(shap...  12.9 us
    unnamed x12, local copies, waits for them, and re-layouts  8.56 us
    ppermute x4, starting transfers between devices, exchange(): return lax.ppermute(face, axis, pairs + [(b, a) for a, b in pairs])  4.51 us
    pallas_call x1, Pallas kernels, local(): pl.pallas_call(functools.partial(frame_kernel, weight), out_shape=(shape(...  3.78 us
    ppermute x4, waiting for transfers between devices, exchange(): return lax.ppermute(face, axis, pairs + [(b, a) for a, b in pairs])  2.29 us
  transfers between devices with their start and end apart: 4, of which 1 were waited for; matrix products, arithmetic and copies ran while one was open for 0% of the time, Pallas kernels for 0%

commit v1 on v0

--- a/solution.py
+++ b/solution.py
@@ -122,19 +122,14 @@
     return part.reshape(rows.shape[0] * SUB, rows.shape[2]).astype(bf16)
 
 
-def window_copies(scalars, factor, window, sems):
-    planes = window.shape[1]
-    return [
+def frame_kernel(weight, scalars, factor, small, blocks, x_even, x_odd, y_even, y_odd, window, total, sems):
+    planes, rows, depth = window.shape[1:]
+    copies = [
         pltpu.make_async_copy(
             factor.at[pl.ds(scalars[0], WINDOW), pl.ds(x, 1)], window.at[:, pl.ds(x, 1)], sems.at[x]
         )
         for x in range(planes)
     ]
-
-
-def frame_kernel(weight, scalars, factor, small, x_even, x_odd, y_even, y_odd, window, total, sems):
-    planes, rows, depth = window.shape[1:]
-    copies = window_copies(scalars, factor, window, sems)
     for copy in copies:
         copy.start()
     sub = iota((WINDOW, planes, depth), 1)
@@ -146,6 +141,7 @@
         products = None
         for half in range(rows // SUB):
             rows_here = block(plane, half)
+            blocks[x, half] = rows_here
             product = dot(rows_here, rows_here, NT)
             products = product if products is None else products + product
         if x == 0:
@@ -172,96 +168,113 @@
     )
 
 
-def project_kernel(
-    weight, scalars, small, factor, x_even, x_odd, y_even, y_odd, diagonal, actuators, sensors,
-    payload, fields, window, rows_all, low_y, high_y, held, gram_a, gram_b, image_a, input_a, sems, out_sems,
+def transform(frame, rows_here):
+    return dot(frame[0], rows_here) + dot(frame[1], rows_here) + dot(frame[2], rows_here)
+
+
+def transform_kernel(
+    weight, small, blocks, actuators, sensors, frame, rows_all, fields, products,
+    act_held, sens_held, gram_a, gram_b, input_a, sems,
 ):
-    planes, rows, depth = window.shape[1:]
-    halves = rows // SUB
-    copies = window_copies(scalars, factor, window, sems)
+    planes, halves = blocks.shape[:2]
+    copies = [
+        pltpu.make_async_copy(actuators, act_held, sems.at[0]),
+        pltpu.make_async_copy(sensors, sens_held, sems.at[1]),
+    ]
     for copy in copies:
         copy.start()
-    frame = expand(split_three(small[:, WINDOW : 2 * WINDOW]))
-
-    def transform(rows_here):
-        return dot(frame[0], rows_here) + dot(frame[1], rows_here) + dot(frame[2], rows_here)
-
+    for at, piece in enumerate(expand(split_three(small[:, WINDOW : 2 * WINDOW]))):
+        frame[at] = piece
+    gram_a[...] = jnp.zeros_like(gram_a)
+    gram_b[...] = jnp.zeros_like(gram_b)
+    input_a[...] = jnp.zeros_like(input_a)
+    for copy in copies:
+        copy.wait()
+
+    def plane_step(x, carry):
+        act_plane, sens_plane = act_held[:, x].astype(f32), sens_held[:, x].astype(f32)
+        for half in range(halves):
+            rows_here = blocks[x, half]
+            inputs = jnp.concatenate([block(act_plane, half), block(sens_plane, half)], axis=0)
+            input_a[...] += dot(rows_here, inputs, NT)
+            value = transform(frame, rows_here)
+            rows_all[x, half] = value
+            high, low = split(value)
+            fields[x, half, 0] = high
+            fields[x, half, 1] = low
+            gram_a[...] += dot(high, high, NT)
+            gram_b[...] += dot(high, low, NT)
+        return carry
+
+    lax.fori_loop(0, planes, plane_step, 0, unroll=True)
+    cross = reduce_rows(gram_b[...])
+    gram = (reduce_rows(gram_a[...]) + cross + cross.T) * weight
+    inputs = mm(small[:, WINDOW : 2 * WINDOW], reduce_rows(input_a[...]) * weight)
+    products[...] = jnp.concatenate(
+        [small[:, :WINDOW], gram, jnp.zeros((WINDOW, WINDOW), f32), inputs,
+         small[:, 2 * WINDOW : 2 * WINDOW + 1], jnp.zeros((WINDOW, 15), f32)], axis=1,
+    )
+
+
+def project_kernel(
+    weight, scalars, frame, rows_all, fields, products, diagonal, x_even, x_odd, y_even, y_odd,
+    payload, images, coefficient, low_x, high_x, low_y, high_y, image_a, sems,
+):
+    planes, halves = rows_all.shape[:2]
+    depth = rows_all.shape[3]
+    tile = (WINDOW, SUB, depth)
+    copy = pltpu.make_async_copy(diagonal, coefficient, sems.at[0])
+    copy.start()
     x_first = scalars[1] == 0
     y_first = scalars[2] == 0
     even, odd = x_even[...].astype(f32), x_odd[...].astype(f32)
     low, high = jnp.where(x_first, odd, even), jnp.where(x_first, even, odd)
     for half in range(halves):
-        rows_all[0, half] = transform(block(low, half))
-        rows_all[planes + 1, half] = transform(block(high, half))
+        low_x[half] = transform(frame, block(low, half))
+        high_x[half] = transform(frame, block(high, half))
     even, odd = y_even[...].astype(f32), y_odd[...].astype(f32)
-    low_y[...] = transform(jnp.where(y_first, odd, even).astype(bf16))
-    high_y[...] = transform(jnp.where(y_first, even, odd).astype(bf16))
-    for copy in copies:
-        copy.wait()
-
-    def transform_plane(x, carry):
-        plane = window[:, x].astype(f32)
-        for half in range(halves):
-            rows_all[x + 1, half] = transform(block(plane, half))
-        return carry
-
-    lax.fori_loop(0, planes, transform_plane, 0)
-    gram_a[...] = jnp.zeros_like(gram_a)
-    gram_b[...] = jnp.zeros_like(gram_b)
+    low_y[...] = transform(frame, jnp.where(y_first, odd, even).astype(bf16))
+    high_y[...] = transform(frame, jnp.where(y_first, even, odd).astype(bf16))
     image_a[...] = jnp.zeros_like(image_a)
-    input_a[...] = jnp.zeros_like(input_a)
-    tile = (WINDOW, SUB, depth)
-
-    def out_copy(x):
-        return pltpu.make_async_copy(held.at[x], fields.at[x], out_sems.at[x])
-
-    def plane_step(x, carry):
+    copy.wait()
+
+    def plane_step(x, below_rows, above_rows):
         sub = iota(tile, 1)
         lane = iota(tile, 2)
-        here = [rows_all[x + 1, half].reshape(tile) for half in range(halves)]
+        here = [rows_all[x, half].reshape(tile) for half in range(halves)]
         up = [pltpu.roll(value, 1, 1) for value in here]
         down = [pltpu.roll(value, SUB - 1, 1) for value in here]
         before = pltpu.roll(low_y[...].reshape(tile), lax.rem(SUB - x, SUB), 1)
         after = pltpu.roll(high_y[...].reshape(tile), lax.rem(2 * SUB - 1 - x, SUB), 1)
-        act_plane, sens_plane = actuators[:, x].astype(f32), sensors[:, x].astype(f32)
         for half in range(halves):
             value = here[half]
             above = jnp.where(sub == 0, before if half == 0 else up[half - 1], up[half])
             below = jnp.where(sub == SUB - 1, after if half == halves - 1 else down[half + 1], down[half])
-            beside = rows_all[x, half].reshape(tile) + rows_all[x + 2, half].reshape(tile)
+            beside = (below_rows(half) + above_rows(half)).reshape(tile)
             beside = beside + above + below
             beside = beside + jnp.where(lane == depth - 1, 0.0, pltpu.roll(value, depth - 1, 2))
             beside = beside + jnp.where(lane == 0, 0.0, pltpu.roll(value, 1, 2))
-            coefficient = 6.0 + diagonal[x, half * SUB : (half + 1) * SUB, :]
-            image = (beside - coefficient[None] * value).reshape(ROWS, depth)
-            field_high, field_low = split(value.reshape(ROWS, depth))
+            scale = 6.0 + coefficient[x, half * SUB : (half + 1) * SUB, :]
+            image = (beside - scale[None] * value).reshape(ROWS, depth)
             image_high, image_low = split(image)
-            held[x, half, 0] = field_high
-            held[x, half, 1] = field_low
-            held[x, half, 2] = image_high
-            held[x, half, 3] = image_low
-            gram_a[...] += dot(field_high, field_high, NT)
-            gram_b[...] += dot(field_high, field_low, NT)
+            images[x, half, 0] = image_high
+            images[x, half, 1] = image_low
+            field_high, field_low = fields[x, half, 0], fields[x, half, 1]
             image_a[...] += (
                 dot(field_high, image_high, NT) + dot(field_low, image_high, NT) + dot(field_high, image_low, NT)
             )
-            inputs = jnp.concatenate([block(act_plane, half), block(sens_plane, half)], axis=0)
-            input_a[...] += dot(field_high, inputs, NT) + dot(field_low, inputs, NT)
-        out_copy(x).start()
+
+    def inner(x, carry):
+        plane_step(x, lambda half: rows_all[x - 1, half], lambda half: rows_all[x + 1, half])
         return carry
 
-    lax.fori_loop(0, planes, plane_step, 0)
-    cross = reduce_rows(gram_b[...])
-    gram = (reduce_rows(gram_a[...]) + cross + cross.T) * weight
+    plane_step(0, lambda half: low_x[half], lambda half: rows_all[1, half])
+    lax.fori_loop(1, planes - 1, inner, 0, unroll=True)
+    plane_step(planes - 1, lambda half: rows_all[planes - 2, half], lambda half: high_x[half])
     image_gram = reduce_rows(image_a[...]) * weight
-    inputs = reduce_rows(input_a[...]) * weight
-    packed = jnp.concatenate(
-        [small[:, :WINDOW], gram, image_gram, inputs, small[:, 2 * WINDOW : 2 * WINDOW + 1],
-         jnp.zeros((WINDOW, 15), f32)], axis=1,
-    )
+    start = 2 * WINDOW
+    packed = jnp.concatenate([products[:, :start], image_gram, products[:, start + WINDOW :]], axis=1)
     payload[...] = jnp.broadcast_to(packed[None], payload.shape)
-    for x in range(planes):
-        out_copy(x).wait()
 
 
 def lyapunov_factor(start, cayley):
@@ -293,14 +306,11 @@
 
 
 def finish_kernel(
-    small, gathered, fields, rotated, residual, riccati_out, gram_out,
-    held, rotated_held, residual_held, sems, out_sems,
+    small, gathered, fields, images, rotated, residual, riccati_out, gram_out,
+    rotated_held, residual_held, out_sems,
 ):
-    planes, halves = held.shape[:2]
+    planes, halves = fields.shape[:2]
     devices = gathered.shape[0]
-    copies = [pltpu.make_async_copy(fields.at[x], held.at[x], sems.at[x]) for x in range(planes)]
-    for copy in copies:
-        copy.start()
     row, column = iota((WINDOW, WINDOW), 0), iota((WINDOW, WINDOW), 1)
     triangle = row <= column
     summed = jnp.sum(gathered[...], axis=0)
@@ -354,8 +364,6 @@
     rotate = mm(riccati, change)
     remove = -mm(riccati, mm(projected, change))
     rotate_high, rotate_low, remove_high, remove_low = expand(split(rotate) + split(remove))
-    for copy in copies:
-        copy.wait()
 
     def out_copies(x):
         return (
@@ -366,8 +374,8 @@
     def plane_step(x, carry):
         turned, left = [], []
         for half in range(halves):
-            field_high, field_low = held[x, half, 0], held[x, half, 1]
-            image_high, image_low = held[x, half, 2], held[x, half, 3]
+            field_high, field_low = fields[x, half, 0], fields[x, half, 1]
+            image_high, image_low = images[x, half, 0], images[x, half, 1]
             depth = field_high.shape[1]
             here = dot(rotate_high, field_high) + dot(rotate_low, field_high) + dot(rotate_high, field_low)
             rest = dot(rotate_high, image_high) + dot(rotate_low, image_high) + dot(rotate_high, image_low)
@@ -380,7 +388,7 @@
             copy.start()
         return carry
 
-    lax.fori_loop(0, planes, plane_step, 0)
+    lax.fori_loop(0, planes, plane_step, 0, unroll=True)
     for x in range(planes):
         for copy in out_copies(x):
             copy.wait()
@@ -395,7 +403,7 @@
 
 vmem = pl.BlockSpec(memory_space=pltpu.VMEM)
 smem = pl.BlockSpec(memory_space=pltpu.SMEM)
-anywhere = pl.BlockSpec(memory_space=pl.ANY)
+hbm = pl.BlockSpec(memory_space=pltpu.HBM)
 
 
 def params(megabytes):
@@ -412,45 +420,67 @@
     scalars = jnp.stack([offset[0], lax.axis_index("gx") % 2, lax.axis_index("gy") % 2]).astype(jnp.int32)
     x_face = shape((WINDOW, rows, depth), bf16)
     y_face = shape((WINDOW * planes, depth), bf16)
-    small, x_even, x_odd, y_even, y_odd = pl.pallas_call(
+    factor, diagonal, actuators, sensors = (
+        pltpu.with_memory_space_constraint(value, pltpu.HBM) for value in (factor, diagonal, actuators, sensors)
+    )
+    pair_shape = (planes, halves, 2, ROWS, depth)
+    rows_shape = (planes, halves, ROWS, depth)
+    small, blocks, x_even, x_odd, y_even, y_odd = pl.pallas_call(
         functools.partial(frame_kernel, weight),
-        out_shape=(shape((WINDOW, 128), f32), x_face, x_face, y_face, y_face),
-        in_specs=[smem, anywhere],
-        out_specs=(vmem,) * 5,
+        out_shape=(shape((WINDOW, 128), f32), shape(rows_shape, bf16), x_face, x_face, y_face, y_face),
+        in_specs=[smem, hbm],
+        out_specs=(vmem,) * 6,
         scratch_shapes=[
             pltpu.VMEM(window_shape, bf16),
             pltpu.VMEM((ROWS, ROWS), f32),
             pltpu.SemaphoreType.DMA((planes,)),
         ],
-        compiler_params=params(24),
+        compiler_params=params(16),
         name="frame",
     )(scalars, factor)
     x_even = exchange(x_even, "gx", False)
     x_odd = exchange(x_odd, "gx", True)
     y_even = exchange(y_even, "gy", False)
     y_odd = exchange(y_odd, "gy", True)
-    fields_shape = (planes, halves, 4, ROWS, depth)
-    payload, fields = pl.pallas_call(
-        functools.partial(project_kernel, weight),
-        out_shape=(shape((devices, WINDOW, 128), f32), shape(fields_shape, bf16)),
-        in_specs=[smem, vmem, anywhere] + [vmem] * 7,
-        out_specs=(vmem, anywhere),
+    frame, rows_all, fields, products = pl.pallas_call(
+        functools.partial(transform_kernel, weight),
+        out_shape=(
+            shape((3, ROWS, ROWS), bf16),
+            shape(rows_shape, f32),
+            shape(pair_shape, bf16),
+            shape((WINDOW, 128), f32),
+        ),
+        in_specs=[vmem, vmem, hbm, hbm],
+        out_specs=(vmem,) * 4,
         scratch_shapes=[
-            pltpu.VMEM(window_shape, bf16),
-            pltpu.VMEM((planes + 2, halves, ROWS, depth), f32),
-            pltpu.VMEM((WINDOW * planes, depth), f32),
-            pltpu.VMEM((WINDOW * planes, depth), f32),
-            pltpu.VMEM(fields_shape, bf16),
-            pltpu.VMEM((ROWS, ROWS), f32),
+            pltpu.VMEM(actuators.shape, bf16),
+            pltpu.VMEM(sensors.shape, bf16),
             pltpu.VMEM((ROWS, ROWS), f32),
             pltpu.VMEM((ROWS, ROWS), f32),
             pltpu.VMEM((ROWS, 16 * SUB), f32),
-            pltpu.SemaphoreType.DMA((planes,)),
-            pltpu.SemaphoreType.DMA((planes,)),
+            pltpu.SemaphoreType.DMA((2,)),
         ],
-        compiler_params=params(40),
+        compiler_params=params(16),
+        cost_estimate=pl.CostEstimate(flops=2 * 10**9, bytes_accessed=8 * 2**20, transcendentals=0),
+        name="transform",
+    )(small, blocks, actuators, sensors)
+    payload, images = pl.pallas_call(
+        functools.partial(project_kernel, weight),
+        out_shape=(shape((devices, WINDOW, 128), f32), shape(pair_shape, bf16)),
+        in_specs=[smem, vmem, vmem, vmem, vmem, hbm] + [vmem] * 4,
+        out_specs=(vmem, vmem),
+        scratch_shapes=[
+            pltpu.VMEM(diagonal.shape, f32),
+            pltpu.VMEM((halves, ROWS, depth), f32),
+            pltpu.VMEM((halves, ROWS, depth), f32),
+            pltpu.VMEM((WINDOW * planes, depth), f32),
+            pltpu.VMEM((WINDOW * planes, depth), f32),
+            pltpu.VMEM((ROWS, ROWS), f32),
+            pltpu.SemaphoreType.DMA((1,)),
+        ],
+        compiler_params=params(16),
         name="project",
-    )(scalars, small, factor, x_even, x_odd, y_even, y_odd, diagonal, actuators, sensors)
+    )(scalars, frame, rows_all, fields, products, diagonal, x_even, x_odd, y_even, y_odd)
     gathered = lax.all_to_all(payload, ("gx", "gy"), 0, 0)
     return pl.pallas_call(
         finish_kernel,
@@ -460,18 +490,16 @@
             shape((WINDOW, WINDOW), f32),
             shape((WINDOW, WINDOW), f32),
         ),
-        in_specs=[vmem, vmem, anywhere],
-        out_specs=(anywhere, anywhere, vmem, vmem),
+        in_specs=[vmem] * 4,
+        out_specs=(hbm, hbm, vmem, vmem),
         scratch_shapes=[
-            pltpu.VMEM(fields_shape, bf16),
             pltpu.VMEM(window_shape, bf16),
             pltpu.VMEM(window_shape, bf16),
-            pltpu.SemaphoreType.DMA((planes,)),
             pltpu.SemaphoreType.DMA((2, planes)),
         ],
-        compiler_params=params(40),
+        compiler_params=params(24),
         name="finish",
-    )(small, gathered, fields)
+    )(small, gathered, fields, images)
 
 
 def solution(mesh):

time: 80.2 us -> 64.1 us (0.80)
  local copies, waits for them, and re-layouts: 8.56 us -> 0 us
  Pallas kernels: 37.3 us -> 34.4 us
  blocking collectives: 25 us -> 22.7 us
  waiting for transfers between devices: 2.29 us -> 0.01 us
    unnamed x12 -> x0, local copies, waits for them, and re-layouts: 8.56 us -> none
    pallas_call x1, Pallas kernels: 12.9 us -> 5.65 us  [local(): pl.pallas_call(functools.partial(project_kernel, weight), out_shape=(shap...]
    pallas_call x0 -> x1, Pallas kernels: none -> 5.49 us  [local(): pl.pallas_call(functools.partial(transform_kernel, weight), out_shape=(sh...]
    all_to_all x1, blocking collectives: 25 us -> 22.7 us  [local(): gathered = lax.all_to_all(payload, ('gx', 'gy'), 0, 0)]
    ppermute x4, waiting for transfers between devices: 2.29 us -> 0.01 us  [exchange(): return lax.ppermute(face, axis, pairs + [(b, a) for a, b in pairs])]
    pallas_call x1, Pallas kernels: 20.7 us -> 18.8 us  [local(): pl.pallas_call(finish_kernel, out_shape=(shape(window_shape, bf16), shape...]
  transfers between devices with their start and end apart: 4 -> 4, of which waited for: 1 -> 0; matrix products, arithmetic and copies ran while one was open for 0% -> 0% of each run, Pallas kernels for 0% -> 9%
where the time goes in v1:
time: 64.1 us; the launch traced here: 63.2 us
  Pallas kernels  34.4 us (54%)
  blocking collectives  22.7 us (35%)
  starting transfers between devices  4.5 us (7%)
  between operations  1.53 us (2%)
    all_to_all x1, blocking collectives, local(): gathered = lax.all_to_all(payload, ('gx', 'gy'), 0, 0)  22.7 us
    pallas_call x1, Pallas kernels, local(): pl.pallas_call(finish_kernel, out_shape=(shape(window_shape, bf16), shape...  18.8 us
    pallas_call x1, Pallas kernels, local(): pl.pallas_call(functools.partial(project_kernel, weight), out_shape=(shap...  5.65 us
    pallas_call x1, Pallas kernels, local(): pl.pallas_call(functools.partial(transform_kernel, weight), out_shape=(sh...  5.49 us
    pallas_call x1, Pallas kernels, local(): pl.pallas_call(functools.partial(frame_kernel, weight), out_shape=(shape(...  4.51 us
    ppermute x4, starting transfers between devices, exchange(): return lax.ppermute(face, axis, pairs + [(b, a) for a, b in pairs])  4.5 us
  transfers between devices with their start and end apart: 4, of which 0 were waited for; matrix products, arithmetic and copies ran while one was open for 0% of the time, Pallas kernels for 9%

profile of v1, /device:TPU:0, one launch (start us, length us, event | category | flops | bytes accessed | tf_op | source)
XLA Modules:
  0.0 63.2 jit_solution(4845225943978146874)
XLA Ops:
  1.3 0.1 pad_add_fusion.scalars
  1.4 4.5 %frame.1 = (f32[32,128]{1,0:T(8,128)S(1)}, bf16[8,2,256,256]{3,2,1,0:T(8,128)(2,1)S(1)}, bf16[32,16,256]{2,1,0:T(8,128)(2,1)S(1)}, bf16[32,16,256]{2,1,0:T(8,128...) custom-call(s32[3]{0:T(128)S(1)} %pad_add_fusion.scalars, bf16[64,8,16,256]{3,2,1,0:T(8,128)(2,1)} %factor.1), custom_call_target="tpu_custom_call" | custom-call | tf_op jit(solution)/shard_map/frame/pallas_call | solution.py:428
  5.9 0.5 collective-permute-start
  6.4 0.7 %collective-permute-start.1 = (bf16[32,16,256]{2,1,0:T(8,128)(2,1)S(1)}, bf16[32,16,256]{2,1,0:T(8,128)(2,1)S(1)}, u32[]{:S(2)}, u32[]{:S(2)}) collective-permute-start(bf16[32,16,256]{2,1,0:T(8,128)(2,1)S(1)} %get-tuple-element.23), channel_id=1, source_target_pairs={{4,8},{12,16},{20,24},{8,4},{16,12},{24,20},{5,9},{13,17},{21,25},... | collective-permute-start | bytes 786440 | tf_op jit(solution)/shard_map/ppermute | solution.py:401
  7.1 2.7 %collective-permute-start.2 = (bf16[256,256]{1,0:T(8,128)(2,1)S(1)}, bf16[256,256]{1,0:T(8,128)(2,1)S(1)}, u32[]{:S(2)}, u32[]{:S(2)}) collective-permute-start(bf16[256,256]{1,0:T(8,128)(2,1)S(1)} %get-tuple-element.24), channel_id=1, source_target_pairs={{0,1},{2,3},{1,0},{3,2},{4,5},{6,7},{5,4},{7,6},{8,9},{10,11},{9,8... | collective-permute-start | bytes 393224 | tf_op jit(solution)/shard_map/ppermute | solution.py:401
  9.7 0.7 %collective-permute-start.3 = (bf16[256,256]{1,0:T(8,128)(2,1)S(1)}, bf16[256,256]{1,0:T(8,128)(2,1)S(1)}, u32[]{:S(2)}, u32[]{:S(2)}) collective-permute-start(bf16[256,256]{1,0:T(8,128)(2,1)S(1)} %get-tuple-element.25), channel_id=1, source_target_pairs={{1,2},{2,1},{5,6},{6,5},{9,10},{10,9},{13,14},{14,13},{17,18},{18,... | collective-permute-start | bytes 393224 | tf_op jit(solution)/shard_map/ppermute | solution.py:401
  10.4 5.5 %transform.1 = (bf16[3,256,256]{2,1,0:T(8,128)(2,1)S(1)}, f32[8,2,256,256]{3,2,1,0:T(8,128)S(1)}, bf16[8,2,2,256,256]{4,3,2,1,0:T(8,128)(2,1)S(1)}, f32[32,128]{1,0:T(8,128)S(1)}) custom-call(f32[32,128]{1,0:T(8,128)S(1)} %get-tuple-element.16.small, bf16[8,2,256,256]{3,2,1,0:T(8,128)(2,1)S(1)} %get-tuple-element.17.blocks, ...), custom_call_target="tpu_custom_call" | custom-call | flops 2000000000 | bytes 8388608 | tf_op jit(solution)/shard_map/transform/pallas_call | solution.py:445
  15.9 0.0 collective-permute-done.2.y_even
  15.9 0.0 collective-permute-done.3.y_odd
  15.9 0.0 collective-permute-done.x_even
  15.9 0.0 collective-permute-done.1.x_odd
  16.0 5.7 %project.1 = (f32[32,32,128]{2,1,0:T(8,128)S(1)}, bf16[8,2,2,256,256]{4,3,2,1,0:T(8,128)(2,1)S(1)}) custom-call(s32[3]{0:T(128)S(1)} %pad_add_fusion.scalars, bf16[3,256,256]{2,1,0:T(8,128)(2,1)S(1)} %get-tuple-element.18.frame, f32[8,2,256,256]{3,2,1,0:T(8,128)S(1)} %get-tuple-element.19.rows_all, ...), custom_call_target="tpu_custom_call" | custom-call | tf_op jit(solution)/shard_map/project/pallas_call | solution.py:467
  21.6 22.7 %all_to_all.5.gathered = f32[32,32,128]{2,1,0:T(8,128)S(1)} all-to-all(f32[32,32,128]{2,1,0:T(8,128)S(1)} %get-tuple-element.26), channel_id=1, replica_groups=mesh['gx'=8,'gy'=4] {'gx','gy'}, dimensions={0} | all-to-all | bytes 1048576 | tf_op jit(solution)/shard_map/all_to_all | solution.py:484
  44.3 18.8 %finish.1 = (bf16[32,8,16,256]{3,2,1,0:T(8,128)(2,1)}, bf16[32,8,16,256]{3,2,1,0:T(8,128)(2,1)}, f32[32,32]{1,0:T(8,128)}, f32[32,32]{1,0:T(8,128)}) custom-call(f32[32,128]{1,0:T(8,128)S(1)} %get-tuple-element.16.small, f32[32,32,128]{2,1,0:T(8,128)S(1)} %all_to_all.5.gathered, bf16[8,2,2,256,256]{4,3,2,1,0:T(8,128)(2,1)S(1)} %get-tuple-element.20.fields, ...), custom_call_target="tpu_custom_call" | custom-call | tf_op jit(solution)/shard_map/finish/pallas_call | solution.py:485
Async XLA Ops:
  5.9 10.0 %collective-permute-start = (bf16[32,16,256]{2,1,0:T(8,128)(2,1)S(1)}, bf16[32,16,256]{2,1,0:T(8,128)(2,1)S(1)}, u32[]{:S(2)}, u32[]{:S(2)}) collective-permute-start(bf16[32,16,256]{2,1,0:T(8,128)(2,1)S(1)} %get-tuple-element.22), channel_id=1, source_target_pairs={{0,4},{8,12},{16,20},{24,28},{4,0},{12,8},{20,16},{28,24},{1,5},{9... | collective-permute-start | bytes 786440 | tf_op jit(solution)/shard_map/ppermute | solution.py:401
  6.4 9.5 %collective-permute-start.1 = (bf16[32,16,256]{2,1,0:T(8,128)(2,1)S(1)}, bf16[32,16,256]{2,1,0:T(8,128)(2,1)S(1)}, u32[]{:S(2)}, u32[]{:S(2)}) collective-permute-start(bf16[32,16,256]{2,1,0:T(8,128)(2,1)S(1)} %get-tuple-element.23), channel_id=1, source_target_pairs={{4,8},{12,16},{20,24},{8,4},{16,12},{24,20},{5,9},{13,17},{21,25},... | collective-permute-start | bytes 786440 | tf_op jit(solution)/shard_map/ppermute | solution.py:401
  7.1 8.8 %collective-permute-start.2 = (bf16[256,256]{1,0:T(8,128)(2,1)S(1)}, bf16[256,256]{1,0:T(8,128)(2,1)S(1)}, u32[]{:S(2)}, u32[]{:S(2)}) collective-permute-start(bf16[256,256]{1,0:T(8,128)(2,1)S(1)} %get-tuple-element.24), channel_id=1, source_target_pairs={{0,1},{2,3},{1,0},{3,2},{4,5},{6,7},{5,4},{7,6},{8,9},{10,11},{9,8... | collective-permute-start | bytes 393224 | tf_op jit(solution)/shard_map/ppermute | solution.py:401
  9.7 6.2 %collective-permute-start.3 = (bf16[256,256]{1,0:T(8,128)(2,1)S(1)}, bf16[256,256]{1,0:T(8,128)(2,1)S(1)}, u32[]{:S(2)}, u32[]{:S(2)}) collective-permute-start(bf16[256,256]{1,0:T(8,128)(2,1)S(1)} %get-tuple-element.25), channel_id=1, source_target_pairs={{1,2},{2,1},{5,6},{6,5},{9,10},{10,9},{13,14},{14,13},{17,18},{18,... | collective-permute-start | bytes 393224 | tf_op jit(solution)/shard_map/ppermute | solution.py:401

commit v2 on v1

v2 whole, which is shorter than its diff:
```python
import functools
import math

import jax
import jax.numpy as jnp
from jax import lax
from jax.experimental import pallas as pl
from jax.experimental.pallas import tpu as pltpu
from jax.sharding import PartitionSpec as P

WINDOW = 32
KLEIN = 3
SMITH = 4
SUB = 8
ROWS = WINDOW * SUB
PANEL = 8
GROUP = 8
SHIFT = 2.0**-15
FLOOR = 1e-30
SECOND_SHIFT = 2.0**-16

f32 = jnp.float32
bf16 = jnp.bfloat16
highest = lax.Precision.HIGHEST
NT = (((1,), (1,)), ((), ()))
NN = (((1,), (0,)), ((), ()))
TN = (((0,), (0,)), ((), ()))


def mm(left, right, dims=NN):
    return lax.dot_general(left, right, dims, precision=highest, preferred_element_type=f32)


def dot(left, right, dims=NN):
    return lax.dot_general(left, right, dims, preferred_element_type=f32)


def split(value):
    high = value.astype(bf16)
    return high, (value - high.astype(f32)).astype(bf16)


def iota(shape, dim):
    return lax.broadcasted_iota(jnp.int32, shape, dim)


def eye(size):
    return (iota((size, size), 0) == iota((size, size), 1)).astype(f32)


def diagonal_of(matrix):
    size = matrix.shape[0]
    mask = iota((size, size), 0) == iota((size, size), 1)
    return jnp.sum(jnp.where(mask, matrix, 0.0), axis=1, keepdims=True)


def eliminate(matrix, full):
    size, width = matrix.shape
    row = iota((size, width), 0)
    for start in range(0, size, PANEL):
        columns = [
            jnp.broadcast_to(matrix[:, start + t : start + t + 1], (size, width)) for t in range(PANEL)
        ]
        for t in range(PANEL):
            at = start + t
            factor = columns[t] * (1.0 / columns[t][at : at + 1, :])
            factor = jnp.where(row != at if full else row > at, factor, 0.0)
            for s in range(t + 1, PANEL):
                columns[s] = columns[s] - factor * columns[s][at : at + 1, :]
            matrix = matrix - factor * matrix[at : at + 1, :]
    return matrix


def cholesky_inverse(gram):
    size = gram.shape[0]
    matrix = eliminate(jnp.concatenate([gram, eye(size)], axis=1), False)
    upper = matrix[:, :size]
    scale = lax.rsqrt(diagonal_of(upper))
    upper = jnp.where(iota((size, size), 0) <= iota((size, size), 1), upper, 0.0)
    return upper * scale, matrix[:, size:] * scale


def solve(square, right):
    size = square.shape[0]
    matrix = eliminate(jnp.concatenate([square, right], axis=1), True)
    return matrix[:, size:] / diagonal_of(matrix[:, :size])


def spread_matrix(count):
    return ((iota((count * SUB, count), 0) >> 3) == iota((count * SUB, count), 1)).astype(bf16)


def same_row(rows, columns):
    return (iota((rows, columns), 0) & 7) == (iota((rows, columns), 1) & 7)


def expand(pieces):
    spread = spread_matrix(WINDOW)
    mask = same_row(ROWS, ROWS)
    out = []
    for piece in pieces:
        tall = jnp.broadcast_to(piece.astype(f32)[:, None, :], (WINDOW, SUB, WINDOW))
        tall = tall.reshape(ROWS, WINDOW).astype(bf16)
        out.append(jnp.where(mask, dot(tall, spread, NT), 0.0).astype(bf16))
    return out


def reduce_rows(total):
    rows, columns = total.shape
    count = columns // SUB
    kept = jnp.where(same_row(rows, columns), total, 0.0)
    kept = jnp.sum(kept.reshape(rows // SUB, SUB, columns), axis=1)
    return mm(kept, spread_matrix(count).astype(f32))


def block(rows, half):
    part = rows[:, half * SUB : (half + 1) * SUB]
    return part.reshape(rows.shape[0] * SUB, rows.shape[2]).astype(bf16)


def frame_kernel(
    weight, scalars, factor, actuators, sensors, diagonal,
    small, blocks, x_even, x_odd, y_even, y_odd, act_held, sens_held, coefficient, window, total, sems, other_sems,
):
    planes, rows, depth = window.shape[1:]
    step = 2
    copies = [
        pltpu.make_async_copy(
            factor.at[pl.ds(scalars[0], WINDOW), pl.ds(x, step)], window.at[:, pl.ds(x, step)], sems.at[x // step]
        )
        for x in range(0, planes, step)
    ]
    others = [
        pltpu.make_async_copy(actuators, act_held, other_sems.at[0]),
        pltpu.make_async_copy(sensors, sens_held, other_sems.at[1]),
        pltpu.make_async_copy(diagonal, coefficient, other_sems.at[2]),
    ]
    for copy in copies + others:
        copy.start()
    sub = iota((WINDOW, planes, depth), 1)
    low_y = jnp.zeros((WINDOW, planes, depth), f32)
    high_y = jnp.zeros((WINDOW, planes, depth), f32)
    for start in range(0, planes, step):
        copies[start // step].wait()
        parts = []
        for x in range(start, start + step):
            plane = window[:, x].astype(f32)
            for half in range(rows // SUB):
                parts.append(block(plane, half))
                blocks[x, half] = parts[-1]
            low_y = jnp.where(sub == x, jnp.broadcast_to(plane[:, :1], low_y.shape), low_y)
            high_y = jnp.where(sub == x, jnp.broadcast_to(plane[:, rows - 1 :], high_y.shape), high_y)
        parts = jnp.concatenate(parts, axis=1)
        if start == 0:
            total[...] = dot(parts, parts, NT)
        else:
            total[...] += dot(parts, parts, NT)
    x_first = scalars[1] == 0
    y_first = scalars[2] == 0
    first, last = window[:, 0], window[:, planes - 1]
    x_even[...] = jnp.where(x_first, last, first)
    x_odd[...] = jnp.where(x_first, first, last)
    low_y = low_y.reshape(WINDOW * planes, depth).astype(bf16)
    high_y = high_y.reshape(WINDOW * planes, depth).astype(bf16)
    y_even[...] = jnp.where(y_first, high_y, low_y)
    y_odd[...] = jnp.where(y_first, low_y, high_y)
    gram = reduce_rows(total[...]) * weight
    on = eye(WINDOW)
    upper, inverse = cholesky_inverse(gram + on * (SHIFT * gram + FLOOR))
    small[...] = jnp.concatenate([upper, inverse, jnp.zeros((WINDOW, 64), f32)], axis=1)
    for copy in others:
        copy.wait()


def transform(frame, rows_here):
    return dot(frame[0], rows_here) + dot(frame[1], rows_here)


def transform_kernel(
    weight, small, blocks, actuators, sensors, frame, rows_all, fields, products, gram_a, gram_b, input_a,
):
    planes, halves = blocks.shape[:2]
    upper = small[:, :WINDOW]
    pieces = split(small[:, WINDOW : 2 * WINDOW])
    for at, piece in enumerate(expand(pieces)):
        frame[at] = piece
    rounded = pieces[0].astype(f32) + pieces[1].astype(f32)
    for _ in range(2):
        upper = upper - mm(mm(upper, rounded, NT) - eye(WINDOW), upper)
    gram_a[...] = jnp.zeros_like(gram_a)
    gram_b[...] = jnp.zeros_like(gram_b)
    input_a[...] = jnp.zeros_like(input_a)

    def plane_step(x, carry):
        for half in range(halves):
            value = transform(frame, blocks[x, half])
            rows_all[x, half] = value
            high, low = split(value)
            fields[x, half, 0] = high
            fields[x, half, 1] = low
        return carry

    def gram_step(x, carry):
        highs = jnp.concatenate([fields[x, half, 0] for half in range(halves)], axis=1)
        lows = jnp.concatenate([fields[x, half, 1] for half in range(halves)], axis=1)
        gram_a[...] += dot(highs, highs, NT)
        gram_b[...] += dot(highs, lows, NT)
        return carry

    def input_step(x, carry):
        act_plane, sens_plane = actuators[:, x].astype(f32), sensors[:, x].astype(f32)
        inputs = [
            jnp.concatenate([block(act_plane, half), block(sens_plane, half)], axis=0) for half in range(halves)
        ]
        rows_here = jnp.concatenate([blocks[x, half] for half in range(halves)], axis=1)
        input_a[...] += dot(rows_here, jnp.concatenate(inputs, axis=1), NT)
        return carry

    lax.fori_loop(0, planes, plane_step, 0, unroll=True)
    lax.fori_loop(0, planes, input_step, 0, unroll=True)
    lax.fori_loop(0, planes, gram_step, 0, unroll=True)
    cross = reduce_rows(gram_b[...])
    gram = (reduce_rows(gram_a[...]) + cross + cross.T) * weight
    second_upper, second = cholesky_inverse(gram + SECOND_SHIFT * eye(WINDOW))
    inputs = mm(second, mm(rounded, reduce_rows(input_a[...]) * weight))
    products[...] = jnp.concatenate(
        [mm(second_upper, upper), second, upper, inputs, jnp.zeros((WINDOW, 16), f32)], axis=1
    )


def pack(matrix):
    return jnp.concatenate([matrix[at : at + SUB] for at in range(0, WINDOW, SUB)], axis=1)


def unpack(stack, start, width):
    parts = [stack[:, :, start + at * width : start + (at + 1) * width] for at in range(WINDOW // SUB)]
    return jnp.concatenate(parts, axis=1).reshape(stack.shape[0] * WINDOW, width)


def project_kernel(
    weight, scalars, frame, rows_all, fields, products, coefficient, x_even, x_odd, y_even, y_odd,
    payload, images, low_x, high_x, low_y, high_y, image_a,
):
    planes, halves = rows_all.shape[:2]
    depth = rows_all.shape[3]
    tile = (WINDOW, SUB, depth)
    x_first = scalars[1] == 0
    y_first = scalars[2] == 0
    even, odd = x_even[...].astype(f32), x_odd[...].astype(f32)
    low, high = jnp.where(x_first, odd, even), jnp.where(x_first, even, odd)
    for half in range(halves):
        low_x[half] = transform(frame, block(low, half))
        high_x[half] = transform(frame, block(high, half))
    even, odd = y_even[...].astype(f32), y_odd[...].astype(f32)
    low_y[...] = transform(frame, jnp.where(y_first, odd, even).astype(bf16))
    high_y[...] = transform(frame, jnp.where(y_first, even, odd).astype(bf16))
    image_a[...] = jnp.zeros_like(image_a)

    def plane_step(x, below_rows, above_rows):
        sub = iota(tile, 1)
        lane = iota(tile, 2)
        here = [rows_all[x, half].reshape(tile) for half in range(halves)]
        up = [pltpu.roll(value, 1, 1) for value in here]
        down = [pltpu.roll(value, SUB - 1, 1) for value in here]
        before = pltpu.roll(low_y[...].reshape(tile), lax.rem(SUB - x, SUB), 1)
        after = pltpu.roll(high_y[...].reshape(tile), lax.rem(2 * SUB - 1 - x, SUB), 1)
        for half in range(halves):
            value = here[half]
            above = jnp.where(sub == 0, before if half == 0 else up[half - 1], up[half])
            below = jnp.where(sub == SUB - 1, after if half == halves - 1 else down[half + 1], down[half])
            beside = (below_rows(half) + above_rows(half)).reshape(tile)
            beside = beside + above + below
            beside = beside + jnp.where(lane == depth - 1, 0.0, pltpu.roll(value, depth - 1, 2))
            beside = beside + jnp.where(lane == 0, 0.0, pltpu.roll(value, 1, 2))
            scale = 6.0 + coefficient[x, half * SUB : (half + 1) * SUB, :]
            image = (beside - scale[None] * value).reshape(ROWS, depth)
            image_high, image_low = split(image)
            images[x, half, 0] = image_high
            images[x, half, 1] = image_low

    def image_step(x, carry):
        left, right = [], []
        for half in range(halves):
            left += [fields[x, half, 0], fields[x, half, 1], fields[x, half, 0]]
            right += [images[x, half, 0], images[x, half, 0], images[x, half, 1]]
        image_a[...] += dot(jnp.concatenate(left, axis=1), jnp.concatenate(right, axis=1), NT)
        return carry

    def inner(x, carry):
        plane_step(x, lambda half: rows_all[x - 1, half], lambda half: rows_all[x + 1, half])
        return carry

    plane_step(0, lambda half: low_x[half], lambda half: rows_all[1, half])
    lax.fori_loop(1, planes - 1, inner, 0, unroll=True)
    plane_step(planes - 1, lambda half: rows_all[planes - 2, half], lambda half: high_x[half])
    lax.fori_loop(0, planes, image_step, 0, unroll=True)
    image_gram = reduce_rows(image_a[...]) * weight
    image_gram = 0.5 * (image_gram + image_gram.T)
    second = products[:, WINDOW : 2 * WINDOW]
    image_gram = mm(mm(second, image_gram), second, NT)
    lower = jnp.where(iota(image_gram.shape, 0) > iota(image_gram.shape, 1), image_gram, 0.0)
    inputs = products[:, 3 * WINDOW : 3 * WINDOW + 16]
    rest = [pack(inputs), pack(diagonal_of(image_gram)), jnp.zeros((SUB, 60), f32)]
    packed = jnp.concatenate([pack(products[:, :WINDOW] + lower), jnp.concatenate(rest, axis=1)], axis=0)
    payload[...] = jnp.broadcast_to(packed[None], payload.shape)


def lyapunov_factor(start, cayley):
    for doubling in range(SMITH):
        start = jnp.concatenate([start, mm(cayley, start)], axis=1)
        if doubling < SMITH - 1:
            cayley = mm(cayley, cayley)
    return start


def riccati_solve(resolvent, inputs):
    count = inputs.shape[1] // 2
    on, on_small = eye(WINDOW), eye(count)
    root = math.sqrt(2.0)
    moved_inputs = mm(resolvent, inputs)
    drive_row, sense_row = moved_inputs[:, :count], moved_inputs[:, count:]
    both = jnp.concatenate([inputs[:, :count], drive_row], axis=1)
    overlap = mm(drive_row, inputs[:, count:], TN)
    first = on - 2.0 * resolvent
    factor = lyapunov_factor(root * sense_row, first)
    for _ in range(KLEIN - 1):
        seen = mm(factor, both, TN)
        moved = mm(resolvent, mm(factor, seen[:, :count]))
        small = on_small + mm(seen[:, count:], seen[:, :count], TN)
        scaled = mm(moved, solve(mm(small, small, TN), small.T))
        start = jnp.concatenate([sense_row - mm(scaled, overlap), scaled], axis=1)
        factor = lyapunov_factor(root * start, first + 2.0 * mm(scaled, drive_row, NT))
    return mm(factor, factor, NT)


def finish_kernel(
    products, gathered, fields, images, rotated, residual, riccati_out, gram_out,
    wide_held, blocks_held, inputs_held, rotated_held, residual_held, out_sems,
):
    planes, halves = fields.shape[:2]
    groups = gathered.shape[0] // GROUP
    wide = GROUP * WINDOW
    row, column = iota((wide, WINDOW), 0) & (WINDOW - 1), iota((wide, WINDOW), 1)
    repeat = ((iota((WINDOW, wide), 1) & (WINDOW - 1)) == iota((WINDOW, wide), 0)).astype(bf16)
    same_block = (iota((wide, wide), 0) // WINDOW) == (iota((wide, wide), 1) // WINDOW)

    def loop(step, totals):
        if groups > 4:
            return lax.fori_loop(0, groups, step, totals)
        for group in range(groups):
            totals = step(group, totals)
        return totals

    def take_group(group, total):
        stack = gathered[pl.ds(group * GROUP, GROUP)]
        mixed = unpack(stack[:, :SUB], 0, WINDOW)
        factors = jnp.where(row <= column, mixed, 0.0).T
        half_diagonal = 0.5 * unpack(stack[:, SUB:], 64, 1)
        image = jnp.where(row > column, mixed, jnp.where(row == column, half_diagonal, 0.0))
        for at, piece in enumerate(split(image)):
            blocks_held[group, at] = jnp.where(same_block, dot(piece, repeat), 0.0).astype(bf16)
        wide_held[group] = factors
        inputs_held[group] = unpack(stack[:, SUB:], 0, 16)
        return total + mm(factors, factors, NT)

    scale = 1.0 / (1.0 + SECOND_SHIFT)
    gram = scale * loop(take_group, jnp.zeros((WINDOW, WINDOW), f32))
    gram_out[...] = gram
    _, first = cholesky_inverse(gram)

    def group_step(group, totals):
        change = mm(first, wide_held[group])
        high, low = split(change)
        image = dot(high, blocks_held[group, 0]) + dot(low, blocks_held[group, 0]) + dot(high, blocks_held[group, 1])
        return (
            totals[0] + mm(change, change, NT),
            totals[1] + mm(image, change, NT),
            totals[2] + mm(change, inputs_held[group]),
        )

    zeros = jnp.zeros((WINDOW, WINDOW), f32)
    gram_second, raw, inputs = loop(group_step, (zeros, zeros, jnp.zeros((WINDOW, 16), f32)))
    gram_second = scale * gram_second
    raw = raw + raw.T
    upper, second = cholesky_inverse(gram_second)
    core = solve(gram_second - raw, eye(WINDOW))
    resolvent = mm(mm(upper, core), upper, NT)
    inputs = mm(second, inputs)
    projected = mm(mm(second, raw), second, NT)
    riccati = riccati_solve(resolvent, inputs)
    riccati_out[...] = riccati
    change = mm(mm(second, first), products[:, 2 * WINDOW : 3 * WINDOW], NT)
    rotate = mm(riccati, change)
    remove = -mm(riccati, mm(projected, change))
    rotate_high, rotate_low, remove_high, remove_low = expand(split(rotate) + split(remove))

    def out_copies(x):
        return (
            pltpu.make_async_copy(rotated_held.at[:, pl.ds(x, 1)], rotated.at[:, pl.ds(x, 1)], out_sems.at[0, x]),
            pltpu.make_async_copy(residual_held.at[:, pl.ds(x, 1)], residual.at[:, pl.ds(x, 1)], out_sems.at[1, x]),
        )

    def plane_step(x, carry):
        turned, left = [], []
        for half in range(halves):
            field_high, field_low = fields[x, half, 0], fields[x, half, 1]
            image_high, image_low = images[x, half, 0], images[x, half, 1]
            depth = field_high.shape[1]
            here = dot(rotate_high, field_high) + dot(rotate_low, field_high) + dot(rotate_high, field_low)
            rest = dot(rotate_high, image_high) + dot(rotate_low, image_high) + dot(rotate_high, image_low)
            rest = rest + (dot(remove_high, field_high) + dot(remove_low, field_high) + dot(remove_high, field_low))
            turned.append(here.reshape(WINDOW, SUB, depth))
            left.append(rest.reshape(WINDOW, SUB, depth))
        rotated_held[:, x] = jnp.concatenate(turned, axis=1).astype(bf16)
        residual_held[:, x] = jnp.concatenate(left, axis=1).astype(bf16)
        for copy in out_copies(x):
            copy.start()
        return carry

    lax.fori_loop(0, planes, plane_step, 0, unroll=True)
    for x in range(planes):
        for copy in out_copies(x):
            copy.wait()


def exchange(face, axis, odd):
    count = lax.axis_size(axis)
    first = 1 if odd else 0
    pairs = [(i, i + 1) for i in range(first, count - 1, 2)]
    return lax.ppermute(face, axis, pairs + [(b, a) for a, b in pairs])


vmem = pl.BlockSpec(memory_space=pltpu.VMEM)
smem = pl.BlockSpec(memory_space=pltpu.SMEM)
hbm = pl.BlockSpec(memory_space=pltpu.HBM)


def params(megabytes):
    return pltpu.CompilerParams(vmem_limit_bytes=megabytes * 2**20)


def local(factor, offset, diagonal, actuators, sensors):
    planes, rows, depth = factor.shape[1:]
    devices = lax.axis_size("gx") * lax.axis_size("gy")
    weight = 1.0 / (planes * rows * depth * devices)
    shape = jax.ShapeDtypeStruct
    window_shape = (WINDOW, planes, rows, depth)
    halves = rows // SUB
    scalars = jnp.stack([offset[0], lax.axis_index("gx") % 2, lax.axis_index("gy") % 2]).astype(jnp.int32)
    x_face = shape((WINDOW, rows, depth), bf16)
    y_face = shape((WINDOW * planes, depth), bf16)
    factor, diagonal, actuators, sensors = (
        pltpu.with_memory_space_constraint(value, pltpu.HBM) for value in (factor, diagonal, actuators, sensors)
    )
    pair_shape = (planes, halves, 2, ROWS, depth)
    rows_shape = (planes, halves, ROWS, depth)
    small, blocks, x_even, x_odd, y_even, y_odd, act_held, sens_held, coefficient = pl.pallas_call(
        functools.partial(frame_kernel, weight),
        out_shape=(
            shape((WINDOW, 128), f32),
            shape(rows_shape, bf16),
            x_face,
            x_face,
            y_face,
            y_face,
            shape(actuators.shape, bf16),
            shape(sensors.shape, bf16),
            shape(diagonal.shape, f32),
        ),
        in_specs=[smem] + [hbm] * 4,
        out_specs=(vmem,) * 9,
        scratch_shapes=[
            pltpu.VMEM(window_shape, bf16),
            pltpu.VMEM((ROWS, ROWS), f32),
            pltpu.SemaphoreType.DMA((planes,)),
            pltpu.SemaphoreType.DMA((3,)),
        ],
        compiler_params=params(16),
        name="frame",
    )(scalars, factor, actuators, sensors, diagonal)
    x_even = exchange(x_even, "gx", False)
    x_odd = exchange(x_odd, "gx", True)
    y_even = exchange(y_even, "gy", False)
    y_odd = exchange(y_odd, "gy", True)
    frame, rows_all, fields, products = pl.pallas_call(
        functools.partial(transform_kernel, weight),
        out_shape=(
            shape((2, ROWS, ROWS), bf16),
            shape(rows_shape, f32),
            shape(pair_shape, bf16),
            shape((WINDOW, 128), f32),
        ),
        in_specs=[vmem] * 4,
        out_specs=(vmem,) * 4,
        scratch_shapes=[
            pltpu.VMEM((ROWS, ROWS), f32),
            pltpu.VMEM((ROWS, ROWS), f32),
            pltpu.VMEM((ROWS, 16 * SUB), f32),
        ],
        compiler_params=params(16),
        cost_estimate=pl.CostEstimate(flops=2 * 10**9, bytes_accessed=8 * 2**20, transcendentals=0),
        name="transform",
    )(small, blocks, act_held, sens_held)
    payload, images = pl.pallas_call(
        functools.partial(project_kernel, weight),
        out_shape=(shape((devices, 2 * SUB, 128), f32), shape(pair_shape, bf16)),
        in_specs=[smem] + [vmem] * 9,
        out_specs=(vmem, vmem),
        scratch_shapes=[
            pltpu.VMEM((halves, ROWS, depth), f32),
            pltpu.VMEM((halves, ROWS, depth), f32),
            pltpu.VMEM((WINDOW * planes, depth), f32),
            pltpu.VMEM((WINDOW * planes, depth), f32),
            pltpu.VMEM((ROWS, ROWS), f32),
        ],
        compiler_params=params(16),
        name="project",
    )(scalars, frame, rows_all, fields, products, coefficient, x_even, x_odd, y_even, y_odd)
    gathered = lax.all_to_all(payload, ("gx", "gy"), 0, 0)
    return pl.pallas_call(
        finish_kernel,
        out_shape=(
            shape(window_shape, bf16),
            shape(window_shape, bf16),
            shape((WINDOW, WINDOW), f32),
            shape((WINDOW, WINDOW), f32),
        ),
        in_specs=[vmem] * 4,
        out_specs=(hbm, hbm, vmem, vmem),
        scratch_shapes=[
            pltpu.VMEM((devices // GROUP, WINDOW, GROUP * WINDOW), f32),
            pltpu.VMEM((devices // GROUP, 2, GROUP * WINDOW, GROUP * WINDOW), bf16),
            pltpu.VMEM((devices // GROUP, GROUP * WINDOW, 16), f32),
            pltpu.VMEM(window_shape, bf16),
            pltpu.VMEM(window_shape, bf16),
            pltpu.SemaphoreType.DMA((2, planes)),
        ],
        compiler_params=params(32),
        name="finish",
    )(products, gathered, fields, images)


def solution(mesh):
    return jax.shard_map(
        local,
        mesh=mesh,
        in_specs=(
            P(None, "gx", "gy", None),
            P(),
            P("gx", "gy", None),
            P(None, "gx", "gy", None),
            P(None, "gx", "gy", None),
        ),
        out_specs=(P(None, "gx", "gy", None), P(None, "gx", "gy", None), P(), P()),
        check_vma=False,
    )
```

time: 64.1 us -> 59 us (0.920); the launches traced: 63.2 us -> 58.8 us
  blocking collectives: 22.7 us -> 18.5 us
    all_to_all x1, blocking collectives: 22.7 us -> 18.5 us  [local(): gathered = lax.all_to_all(payload, ('gx', 'gy'), 0, 0)]
where the time goes in v2:
time: 59 us; the launch traced here: 58.8 us
  Pallas kernels  34.1 us (58%)
  blocking collectives  18.5 us (31%)
  starting transfers between devices  4.5 us (8%)
  between operations  1.51 us (3%)
    all_to_all x1, blocking collectives, local(): gathered = lax.all_to_all(payload, ('gx', 'gy'), 0, 0)  18.5 us
    pallas_call x1, Pallas kernels, local(): pl.pallas_call(finish_kernel, out_shape=(shape(window_shape, bf16), shape...  18.5 us
    pallas_call x1, Pallas kernels, local(): pl.pallas_call(functools.partial(project_kernel, weight), out_shape=(shap...  5.92 us
    pallas_call x1, Pallas kernels, local(): pl.pallas_call(functools.partial(transform_kernel, weight), out_shape=(sh...  5.22 us
    pallas_call x1, Pallas kernels, local(): pl.pallas_call(functools.partial(frame_kernel, weight), out_shape=(shape(...  4.51 us
    ppermute x4, starting transfers between devices, exchange(): return lax.ppermute(face, axis, pairs + [(b, a) for a, b in pairs])  4.5 us
  transfers between devices with their start and end apart: 4, of which 0 were waited for; matrix products, arithmetic and copies ran while one was open for 0% of the time, Pallas kernels for 9%

profile of v2, /device:TPU:0, one launch (start us, length us, event | category | flops | bytes accessed | tf_op | source)
XLA Modules:
  0.0 58.8 jit_solution(16002239614894218220)
XLA Ops:
  1.3 0.1 pad_add_fusion.scalars
  1.4 4.5 %frame.1 = (f32[32,128]{1,0:T(8,128)S(1)}, bf16[8,2,256,256]{3,2,1,0:T(8,128)(2,1)S(1)}, bf16[32,16,256]{2,1,0:T(8,128)(2,1)S(1)}, bf16[32,16,256]{2,1,0:T(8,128...) custom-call(s32[3]{0:T(128)S(1)} %pad_add_fusion.scalars, ...), custom_call_target="tpu_custom_call" | custom-call | tf_op jit(solution)/shard_map/frame/pallas_call | solution.py:457
  5.9 0.5 collective-permute-start
  6.4 0.7 %collective-permute-start.1 = (bf16[32,16,256]{2,1,0:T(8,128)(2,1)S(1)}, bf16[32,16,256]{2,1,0:T(8,128)(2,1)S(1)}, u32[]{:S(2)}, u32[]{:S(2)}) collective-permute-start(bf16[32,16,256]{2,1,0:T(8,128)(2,1)S(1)} %get-tuple-element.29), channel_id=1, source_target_pairs={{4,8},{12,16},{20,24},{8,4},{16,12},{24,20},{5,9},{13,17},{21,25},... | collective-permute-start | bytes 786440 | tf_op jit(solution)/shard_map/ppermute | solution.py:430
  7.1 2.7 %collective-permute-start.2 = (bf16[256,256]{1,0:T(8,128)(2,1)S(1)}, bf16[256,256]{1,0:T(8,128)(2,1)S(1)}, u32[]{:S(2)}, u32[]{:S(2)}) collective-permute-start(bf16[256,256]{1,0:T(8,128)(2,1)S(1)} %get-tuple-element.30), channel_id=1, source_target_pairs={{0,1},{2,3},{1,0},{3,2},{4,5},{6,7},{5,4},{7,6},{8,9},{10,11},{9,8... | collective-permute-start | bytes 393224 | tf_op jit(solution)/shard_map/ppermute | solution.py:430
  9.7 0.7 %collective-permute-start.3 = (bf16[256,256]{1,0:T(8,128)(2,1)S(1)}, bf16[256,256]{1,0:T(8,128)(2,1)S(1)}, u32[]{:S(2)}, u32[]{:S(2)}) collective-permute-start(bf16[256,256]{1,0:T(8,128)(2,1)S(1)} %get-tuple-element.31), channel_id=1, source_target_pairs={{1,2},{2,1},{5,6},{6,5},{9,10},{10,9},{13,14},{14,13},{17,18},{18,... | collective-permute-start | bytes 393224 | tf_op jit(solution)/shard_map/ppermute | solution.py:430
  10.4 5.2 %transform.1 = (bf16[2,256,256]{2,1,0:T(8,128)(2,1)S(1)}, f32[8,2,256,256]{3,2,1,0:T(8,128)S(1)}, bf16[8,2,2,256,256]{4,3,2,1,0:T(8,128)(2,1)S(1)}, f32[32,128]{1,0:T(8,128)S(1)}) custom-call(f32[32,128]{1,0:T(8,128)S(1)} %get-tuple-element.19.small, bf16[8,2,256,256]{3,2,1,0:T(8,128)(2,1)S(1)} %get-tuple-element.20.blocks, ...), custom_call_target="tpu_custom_call" | custom-call | flops 2000000000 | bytes 8388608 | tf_op jit(solution)/shard_map/transform/pallas_call | solution.py:485
  15.6 0.0 collective-permute-done.2.y_even
  15.6 0.0 collective-permute-done.3.y_odd
  15.7 0.0 collective-permute-done.x_even
  15.7 0.0 collective-permute-done.1.x_odd
  15.7 5.9 %project.1 = (f32[32,16,128]{2,1,0:T(8,128)S(1)}, bf16[8,2,2,256,256]{4,3,2,1,0:T(8,128)(2,1)S(1)}) custom-call(s32[3]{0:T(128)S(1)} %pad_add_fusion.scalars, bf16[2,256,256]{2,1,0:T(8,128)(2,1)S(1)} %get-tuple-element.24.frame, f32[8,2,256,256]{3,2,1,0:T(8,128)S(1)} %get-tuple-element.25.rows_all, ...), custom_call_target="tpu_custom_call" | custom-call | tf_op jit(solution)/shard_map/project/pallas_call | solution.py:504
  21.6 18.5 %all_to_all.5.gathered = f32[32,16,128]{2,1,0:T(8,128)S(1)} all-to-all(f32[32,16,128]{2,1,0:T(8,128)S(1)} %get-tuple-element.32), channel_id=1, replica_groups=mesh['gx'=8,'gy'=4] {'gx','gy'}, dimensions={0} | all-to-all | bytes 524288 | tf_op jit(solution)/shard_map/all_to_all | solution.py:519
  40.1 18.5 %finish.1 = (bf16[32,8,16,256]{3,2,1,0:T(8,128)(2,1)}, bf16[32,8,16,256]{3,2,1,0:T(8,128)(2,1)}, f32[32,32]{1,0:T(8,128)}, f32[32,32]{1,0:T(8,128)}) custom-call(f32[32,128]{1,0:T(8,128)S(1)} %get-tuple-element.23.products, f32[32,16,128]{2,1,0:T(8,128)S(1)} %all_to_all.5.gathered, bf16[8,2,2,256,256]{4,3,2,1,0:T(8,128)(2,1)S(1)} %get-tuple-element.26.fields, ...), custom_call_target="tpu_custom_call" | custom-call | tf_op jit(solution)/shard_map/finish/pallas_call | solution.py:520
Async XLA Ops:
  5.9 9.8 %collective-permute-start = (bf16[32,16,256]{2,1,0:T(8,128)(2,1)S(1)}, bf16[32,16,256]{2,1,0:T(8,128)(2,1)S(1)}, u32[]{:S(2)}, u32[]{:S(2)}) collective-permute-start(bf16[32,16,256]{2,1,0:T(8,128)(2,1)S(1)} %get-tuple-element.28), channel_id=1, source_target_pairs={{0,4},{8,12},{16,20},{24,28},{4,0},{12,8},{20,16},{28,24},{1,5},{9... | collective-permute-start | bytes 786440 | tf_op jit(solution)/shard_map/ppermute | solution.py:430
  6.4 9.3 %collective-permute-start.1 = (bf16[32,16,256]{2,1,0:T(8,128)(2,1)S(1)}, bf16[32,16,256]{2,1,0:T(8,128)(2,1)S(1)}, u32[]{:S(2)}, u32[]{:S(2)}) collective-permute-start(bf16[32,16,256]{2,1,0:T(8,128)(2,1)S(1)} %get-tuple-element.29), channel_id=1, source_target_pairs={{4,8},{12,16},{20,24},{8,4},{16,12},{24,20},{5,9},{13,17},{21,25},... | collective-permute-start | bytes 786440 | tf_op jit(solution)/shard_map/ppermute | solution.py:430
  7.1 8.6 %collective-permute-start.2 = (bf16[256,256]{1,0:T(8,128)(2,1)S(1)}, bf16[256,256]{1,0:T(8,128)(2,1)S(1)}, u32[]{:S(2)}, u32[]{:S(2)}) collective-permute-start(bf16[256,256]{1,0:T(8,128)(2,1)S(1)} %get-tuple-element.30), channel_id=1, source_target_pairs={{0,1},{2,3},{1,0},{3,2},{4,5},{6,7},{5,4},{7,6},{8,9},{10,11},{9,8... | collective-permute-start | bytes 393224 | tf_op jit(solution)/shard_map/ppermute | solution.py:430
  9.7 5.9 %collective-permute-start.3 = (bf16[256,256]{1,0:T(8,128)(2,1)S(1)}, bf16[256,256]{1,0:T(8,128)(2,1)S(1)}, u32[]{:S(2)}, u32[]{:S(2)}) collective-permute-start(bf16[256,256]{1,0:T(8,128)(2,1)S(1)} %get-tuple-element.31), channel_id=1, source_target_pairs={{1,2},{2,1},{5,6},{6,5},{9,10},{10,9},{13,14},{14,13},{17,18},{18,... | collective-permute-start | bytes 393224 | tf_op jit(solution)/shard_map/ppermute | solution.py:430

commit v3 on v2

--- a/solution.py
+++ b/solution.py
@@ -38,6 +38,12 @@
 def split(value):
     high = value.astype(bf16)
     return high, (value - high.astype(f32)).astype(bf16)
+
+
+def mm_three(left, right, dims=NN):
+    left_high, left_low = split(left)
+    right_high, right_low = split(right)
+    return dot(left_high, right_high, dims) + (dot(left_high, right_low, dims) + dot(left_low, right_high, dims))
 
 
 def iota(shape, dim):
@@ -191,34 +197,34 @@
     gram_b[...] = jnp.zeros_like(gram_b)
     input_a[...] = jnp.zeros_like(input_a)
 
-    def plane_step(x, carry):
+    def plane_step(x):
         for half in range(halves):
             value = transform(frame, blocks[x, half])
             rows_all[x, half] = value
             high, low = split(value)
             fields[x, half, 0] = high
             fields[x, half, 1] = low
-        return carry
-
-    def gram_step(x, carry):
+
+    def gram_step(x):
         highs = jnp.concatenate([fields[x, half, 0] for half in range(halves)], axis=1)
         lows = jnp.concatenate([fields[x, half, 1] for half in range(halves)], axis=1)
         gram_a[...] += dot(highs, highs, NT)
         gram_b[...] += dot(highs, lows, NT)
-        return carry
-
-    def input_step(x, carry):
+
+    def input_step(x):
         act_plane, sens_plane = actuators[:, x].astype(f32), sensors[:, x].astype(f32)
         inputs = [
             jnp.concatenate([block(act_plane, half), block(sens_plane, half)], axis=0) for half in range(halves)
         ]
         rows_here = jnp.concatenate([blocks[x, half] for half in range(halves)], axis=1)
         input_a[...] += dot(rows_here, jnp.concatenate(inputs, axis=1), NT)
-        return carry
-
-    lax.fori_loop(0, planes, plane_step, 0, unroll=True)
-    lax.fori_loop(0, planes, input_step, 0, unroll=True)
-    lax.fori_loop(0, planes, gram_step, 0, unroll=True)
+
+    for x in range(planes + 1):
+        if x < planes:
+            plane_step(x)
+            input_step(x)
+        if x > 0:
+            gram_step(x - 1)
     cross = reduce_rows(gram_b[...])
     gram = (reduce_rows(gram_a[...]) + cross + cross.T) * weight
     second_upper, second = cholesky_inverse(gram + SECOND_SHIFT * eye(WINDOW))
@@ -248,9 +254,11 @@
     y_first = scalars[2] == 0
     even, odd = x_even[...].astype(f32), x_odd[...].astype(f32)
     low, high = jnp.where(x_first, odd, even), jnp.where(x_first, even, odd)
-    for half in range(halves):
-        low_x[half] = transform(frame, block(low, half))
-        high_x[half] = transform(frame, block(high, half))
+
+    def face_step(rows_out, face):
+        for half in range(halves):
+            rows_out[half] = transform(frame, block(face, half))
+
     even, odd = y_even[...].astype(f32), y_odd[...].astype(f32)
     low_y[...] = transform(frame, jnp.where(y_first, odd, even).astype(bf16))
     high_y[...] = transform(frame, jnp.where(y_first, even, odd).astype(bf16))
@@ -278,22 +286,29 @@
             images[x, half, 0] = image_high
             images[x, half, 1] = image_low
 
-    def image_step(x, carry):
+    def image_step(x):
         left, right = [], []
         for half in range(halves):
             left += [fields[x, half, 0], fields[x, half, 1], fields[x, half, 0]]
             right += [images[x, half, 0], images[x, half, 0], images[x, half, 1]]
         image_a[...] += dot(jnp.concatenate(left, axis=1), jnp.concatenate(right, axis=1), NT)
-        return carry
-
-    def inner(x, carry):
+
+    def inner(x):
         plane_step(x, lambda half: rows_all[x - 1, half], lambda half: rows_all[x + 1, half])
-        return carry
-
+
+    inner(1)
+    face_step(low_x, low)
+    inner(2)
+    image_step(1)
+    face_step(high_x, high)
+    for x in range(3, planes - 1):
+        inner(x)
+        image_step(x - 1)
     plane_step(0, lambda half: low_x[half], lambda half: rows_all[1, half])
-    lax.fori_loop(1, planes - 1, inner, 0, unroll=True)
+    image_step(planes - 2)
     plane_step(planes - 1, lambda half: rows_all[planes - 2, half], lambda half: high_x[half])
-    lax.fori_loop(0, planes, image_step, 0, unroll=True)
+    image_step(0)
+    image_step(planes - 1)
     image_gram = reduce_rows(image_a[...]) * weight
     image_gram = 0.5 * (image_gram + image_gram.T)
     second = products[:, WINDOW : 2 * WINDOW]
@@ -305,37 +320,46 @@
     payload[...] = jnp.broadcast_to(packed[None], payload.shape)
 
 
-def lyapunov_factor(start, cayley):
+def lyapunov_factor(start, cayley, beside):
     for doubling in range(SMITH):
-        start = jnp.concatenate([start, mm(cayley, start)], axis=1)
+        grown = mm_three(start, cayley)
         if doubling < SMITH - 1:
-            cayley = mm(cayley, cayley)
+            cayley = mm_three(cayley, cayley)
+        start = jnp.concatenate([start, grown], axis=0)
+        beside()
     return start
 
 
-def riccati_solve(resolvent, inputs):
+def riccati_solve(resolvent, inputs, beside):
     count = inputs.shape[1] // 2
     on, on_small = eye(WINDOW), eye(count)
     root = math.sqrt(2.0)
-    moved_inputs = mm(resolvent, inputs)
-    drive_row, sense_row = moved_inputs[:, :count], moved_inputs[:, count:]
-    both = jnp.concatenate([inputs[:, :count], drive_row], axis=1)
-    overlap = mm(drive_row, inputs[:, count:], TN)
+    moved_rows = mm(inputs, resolvent, TN)
+    sense_row = moved_rows[count:]
+    drive_column = mm(resolvent, inputs[:, :count])
+    both = jnp.concatenate([inputs[:, :count].T, moved_rows[:count]], axis=0)
+    overlap = mm(inputs[:, count:], drive_column, TN)
     first = on - 2.0 * resolvent
-    factor = lyapunov_factor(root * sense_row, first)
+    beside()
+    factor = lyapunov_factor(root * sense_row, first, beside)
     for _ in range(KLEIN - 1):
-        seen = mm(factor, both, TN)
-        moved = mm(resolvent, mm(factor, seen[:, :count]))
-        small = on_small + mm(seen[:, count:], seen[:, :count], TN)
-        scaled = mm(moved, solve(mm(small, small, TN), small.T))
-        start = jnp.concatenate([sense_row - mm(scaled, overlap), scaled], axis=1)
-        factor = lyapunov_factor(root * start, first + 2.0 * mm(scaled, drive_row, NT))
-    return mm(factor, factor, NT)
+        seen = mm(both, factor, NT)
+        beside()
+        small = on_small + mm(seen[count:], seen[:count], NT)
+        moved = mm(seen[:count], factor)
+        normal = mm(small, small, NT)
+        moved = mm(moved, resolvent)
+        beside()
+        beside()
+        scaled = mm(solve(normal, small), moved)
+        start = jnp.concatenate([sense_row - mm(overlap, scaled), scaled], axis=0)
+        factor = lyapunov_factor(root * start, first + 2.0 * mm(drive_column, scaled), beside)
+    return mm(factor, factor, TN)
 
 
 def finish_kernel(
     products, gathered, fields, images, rotated, residual, riccati_out, gram_out,
-    wide_held, blocks_held, inputs_held, rotated_held, residual_held, out_sems,
+    wide_held, blocks_held, inputs_held, prepared, rotated_held, residual_held, out_sems,
 ):
     planes, halves = fields.shape[:2]
     groups = gathered.shape[0] // GROUP
@@ -373,9 +397,9 @@
         high, low = split(change)
         image = dot(high, blocks_held[group, 0]) + dot(low, blocks_held[group, 0]) + dot(high, blocks_held[group, 1])
         return (
-            totals[0] + mm(change, change, NT),
-            totals[1] + mm(image, change, NT),
-            totals[2] + mm(change, inputs_held[group]),
+            totals[0] + mm_three(change, change, NT),
+            totals[1] + mm_three(image, change, NT),
+            totals[2] + mm_three(change, inputs_held[group]),
         )
 
     zeros = jnp.zeros((WINDOW, WINDOW), f32)
@@ -384,15 +408,31 @@
     raw = raw + raw.T
     upper, second = cholesky_inverse(gram_second)
     core = solve(gram_second - raw, eye(WINDOW))
-    resolvent = mm(mm(upper, core), upper, NT)
-    inputs = mm(second, inputs)
-    projected = mm(mm(second, raw), second, NT)
-    riccati = riccati_solve(resolvent, inputs)
+    resolvent = mm_three(mm_three(upper, core), upper, NT)
+    inputs = mm_three(second, inputs)
+    projected = mm_three(mm_three(second, raw), second, NT)
+    change = mm_three(mm(second, first), products[:, 2 * WINDOW : 3 * WINDOW], NT)
+    remove = -mm_three(projected, change)
+    change_high, change_low, remove_high, remove_low = expand(split(change) + split(remove))
+    tasks = [(x, half) for x in range(planes) for half in range(halves)]
+
+    def prepare():
+        if not tasks:
+            return
+        x, half = tasks.pop(0)
+        field_high, field_low = fields[x, half, 0], fields[x, half, 1]
+        image_high, image_low = images[x, half, 0], images[x, half, 1]
+        basis = dot(change_high, field_high) + dot(change_low, field_high) + dot(change_high, field_low)
+        rest = dot(change_high, image_high) + dot(change_low, image_high) + dot(change_high, image_low)
+        rest = rest + (dot(remove_high, field_high) + dot(remove_low, field_high) + dot(remove_high, field_low))
+        for at, piece in enumerate(split(basis) + split(rest)):
+            prepared[x, half, at] = piece
+
+    riccati = riccati_solve(resolvent, inputs, prepare)
     riccati_out[...] = riccati
-    change = mm(mm(second, first), products[:, 2 * WINDOW : 3 * WINDOW], NT)
-    rotate = mm(riccati, change)
-    remove = -mm(riccati, mm(projected, change))
-    rotate_high, rotate_low, remove_high, remove_low = expand(split(rotate) + split(remove))
+    while tasks:
+        prepare()
+    rotate_high, rotate_low = expand(split(riccati))
 
     def out_copies(x):
         return (
@@ -403,12 +443,10 @@
     def plane_step(x, carry):
         turned, left = [], []
         for half in range(halves):
-            field_high, field_low = fields[x, half, 0], fields[x, half, 1]
-            image_high, image_low = images[x, half, 0], images[x, half, 1]
-            depth = field_high.shape[1]
-            here = dot(rotate_high, field_high) + dot(rotate_low, field_high) + dot(rotate_high, field_low)
-            rest = dot(rotate_high, image_high) + dot(rotate_low, image_high) + dot(rotate_high, image_low)
-            rest = rest + (dot(remove_high, field_high) + dot(remove_low, field_high) + dot(remove_high, field_low))
+            basis_high, basis_low, rest_high, rest_low = (prepared[x, half, at] for at in range(4))
+            depth = basis_high.shape[1]
+            here = dot(rotate_high, basis_high) + dot(rotate_low, basis_high) + dot(rotate_high, basis_low)
+            rest = dot(rotate_high, rest_high) + dot(rotate_low, rest_high) + dot(rotate_high, rest_low)
             turned.append(here.reshape(WINDOW, SUB, depth))
             left.append(rest.reshape(WINDOW, SUB, depth))
         rotated_held[:, x] = jnp.concatenate(turned, axis=1).astype(bf16)
@@ -531,6 +569,7 @@
             pltpu.VMEM((devices // GROUP, WINDOW, GROUP * WINDOW), f32),
             pltpu.VMEM((devices // GROUP, 2, GROUP * WINDOW, GROUP * WINDOW), bf16),
             pltpu.VMEM((devices // GROUP, GROUP * WINDOW, 16), f32),
+            pltpu.VMEM((planes, halves, 4, ROWS, depth), bf16),
             pltpu.VMEM(window_shape, bf16),
             pltpu.VMEM(window_shape, bf16),
             pltpu.SemaphoreType.DMA((2, planes)),

time: 59 us -> 57 us (0.966)
  Pallas kernels: 34.1 us -> 32.2 us
    pallas_call x1, Pallas kernels: 18.5 us -> 17.3 us  [local(): pl.pallas_call(finish_kernel, out_shape=(shape(window_shape, bf16), shape...]
    pallas_call x1, Pallas kernels: 5.92 us -> 5.23 us  [local(): pl.pallas_call(functools.partial(project_kernel, weight), out_shape=(shap...]
where the time goes in v3:
time: 57 us; the launch traced here: 56.8 us
  Pallas kernels  32.2 us (56%)
  blocking collectives  18.5 us (32%)
  starting transfers between devices  4.5 us (8%)
  between operations  1.51 us (3%)
    all_to_all x1, blocking collectives, local(): gathered = lax.all_to_all(payload, ('gx', 'gy'), 0, 0)  18.5 us
    pallas_call x1, Pallas kernels, local(): pl.pallas_call(finish_kernel, out_shape=(shape(window_shape, bf16), shape...  17.3 us
    pallas_call x1, Pallas kernels, local(): pl.pallas_call(functools.partial(project_kernel, weight), out_shape=(shap...  5.23 us
    pallas_call x1, Pallas kernels, local(): pl.pallas_call(functools.partial(transform_kernel, weight), out_shape=(sh...  5.13 us
    pallas_call x1, Pallas kernels, local(): pl.pallas_call(functools.partial(frame_kernel, weight), out_shape=(shape(...  4.51 us
    ppermute x4, starting transfers between devices, exchange(): return lax.ppermute(face, axis, pairs + [(b, a) for a, b in pairs])  4.5 us
  transfers between devices with their start and end apart: 4, of which 0 were waited for; matrix products, arithmetic and copies ran while one was open for 0% of the time, Pallas kernels for 9%

profile of v3, /device:TPU:0, one launch (start us, length us, event | category | flops | bytes accessed | tf_op | source)
XLA Modules:
  0.0 56.8 jit_solution(8891668867905101710)
XLA Ops:
  1.3 0.1 pad_add_fusion.scalars
  1.4 4.5 %frame.1 = (f32[32,128]{1,0:T(8,128)S(1)}, bf16[8,2,256,256]{3,2,1,0:T(8,128)(2,1)S(1)}, bf16[32,16,256]{2,1,0:T(8,128)(2,1)S(1)}, bf16[32,16,256]{2,1,0:T(8,128...) custom-call(s32[3]{0:T(128)S(1)} %pad_add_fusion.scalars, ...), custom_call_target="tpu_custom_call" | custom-call | tf_op jit(solution)/shard_map/frame/pallas_call | solution.py:495
  5.9 0.5 collective-permute-start
  6.4 0.7 %collective-permute-start.1 = (bf16[32,16,256]{2,1,0:T(8,128)(2,1)S(1)}, bf16[32,16,256]{2,1,0:T(8,128)(2,1)S(1)}, u32[]{:S(2)}, u32[]{:S(2)}) collective-permute-start(bf16[32,16,256]{2,1,0:T(8,128)(2,1)S(1)} %get-tuple-element.29), channel_id=1, source_target_pairs={{4,8},{12,16},{20,24},{8,4},{16,12},{24,20},{5,9},{13,17},{21,25},... | collective-permute-start | bytes 786440 | tf_op jit(solution)/shard_map/ppermute | solution.py:468
  7.1 2.7 %collective-permute-start.2 = (bf16[256,256]{1,0:T(8,128)(2,1)S(1)}, bf16[256,256]{1,0:T(8,128)(2,1)S(1)}, u32[]{:S(2)}, u32[]{:S(2)}) collective-permute-start(bf16[256,256]{1,0:T(8,128)(2,1)S(1)} %get-tuple-element.30), channel_id=1, source_target_pairs={{0,1},{2,3},{1,0},{3,2},{4,5},{6,7},{5,4},{7,6},{8,9},{10,11},{9,8... | collective-permute-start | bytes 393224 | tf_op jit(solution)/shard_map/ppermute | solution.py:468
  9.7 0.7 %collective-permute-start.3 = (bf16[256,256]{1,0:T(8,128)(2,1)S(1)}, bf16[256,256]{1,0:T(8,128)(2,1)S(1)}, u32[]{:S(2)}, u32[]{:S(2)}) collective-permute-start(bf16[256,256]{1,0:T(8,128)(2,1)S(1)} %get-tuple-element.31), channel_id=1, source_target_pairs={{1,2},{2,1},{5,6},{6,5},{9,10},{10,9},{13,14},{14,13},{17,18},{18,... | collective-permute-start | bytes 393224 | tf_op jit(solution)/shard_map/ppermute | solution.py:468
  10.4 5.1 %transform.1 = (bf16[2,256,256]{2,1,0:T(8,128)(2,1)S(1)}, f32[8,2,256,256]{3,2,1,0:T(8,128)S(1)}, bf16[8,2,2,256,256]{4,3,2,1,0:T(8,128)(2,1)S(1)}, f32[32,128]{1,0:T(8,128)S(1)}) custom-call(f32[32,128]{1,0:T(8,128)S(1)} %get-tuple-element.19.small, bf16[8,2,256,256]{3,2,1,0:T(8,128)(2,1)S(1)} %get-tuple-element.20.blocks, ...), custom_call_target="tpu_custom_call" | custom-call | flops 2000000000 | bytes 8388608 | tf_op jit(solution)/shard_map/transform/pallas_call | solution.py:523
  15.5 0.0 collective-permute-done.2.y_even
  15.5 0.0 collective-permute-done.3.y_odd
  15.6 0.0 collective-permute-done.x_even
  15.6 0.0 collective-permute-done.1.x_odd
  15.6 5.2 %project.1 = (f32[32,16,128]{2,1,0:T(8,128)S(1)}, bf16[8,2,2,256,256]{4,3,2,1,0:T(8,128)(2,1)S(1)}) custom-call(s32[3]{0:T(128)S(1)} %pad_add_fusion.scalars, bf16[2,256,256]{2,1,0:T(8,128)(2,1)S(1)} %get-tuple-element.24.frame, f32[8,2,256,256]{3,2,1,0:T(8,128)S(1)} %get-tuple-element.25.rows_all, ...), custom_call_target="tpu_custom_call" | custom-call | tf_op jit(solution)/shard_map/project/pallas_call | solution.py:542
  20.8 18.5 %all_to_all.5.gathered = f32[32,16,128]{2,1,0:T(8,128)S(1)} all-to-all(f32[32,16,128]{2,1,0:T(8,128)S(1)} %get-tuple-element.32), channel_id=1, replica_groups=mesh['gx'=8,'gy'=4] {'gx','gy'}, dimensions={0} | all-to-all | bytes 524288 | tf_op jit(solution)/shard_map/all_to_all | solution.py:557
  39.3 17.3 %finish.1 = (bf16[32,8,16,256]{3,2,1,0:T(8,128)(2,1)}, bf16[32,8,16,256]{3,2,1,0:T(8,128)(2,1)}, f32[32,32]{1,0:T(8,128)}, f32[32,32]{1,0:T(8,128)}) custom-call(f32[32,128]{1,0:T(8,128)S(1)} %get-tuple-element.23.products, f32[32,16,128]{2,1,0:T(8,128)S(1)} %all_to_all.5.gathered, bf16[8,2,2,256,256]{4,3,2,1,0:T(8,128)(2,1)S(1)} %get-tuple-element.26.fields, ...), custom_call_target="tpu_custom_call" | custom-call | tf_op jit(solution)/shard_map/finish/pallas_call | solution.py:558
Async XLA Ops:
  5.9 9.7 %collective-permute-start = (bf16[32,16,256]{2,1,0:T(8,128)(2,1)S(1)}, bf16[32,16,256]{2,1,0:T(8,128)(2,1)S(1)}, u32[]{:S(2)}, u32[]{:S(2)}) collective-permute-start(bf16[32,16,256]{2,1,0:T(8,128)(2,1)S(1)} %get-tuple-element.28), channel_id=1, source_target_pairs={{0,4},{8,12},{16,20},{24,28},{4,0},{12,8},{20,16},{28,24},{1,5},{9... | collective-permute-start | bytes 786440 | tf_op jit(solution)/shard_map/ppermute | solution.py:468
  6.4 9.2 %collective-permute-start.1 = (bf16[32,16,256]{2,1,0:T(8,128)(2,1)S(1)}, bf16[32,16,256]{2,1,0:T(8,128)(2,1)S(1)}, u32[]{:S(2)}, u32[]{:S(2)}) collective-permute-start(bf16[32,16,256]{2,1,0:T(8,128)(2,1)S(1)} %get-tuple-element.29), channel_id=1, source_target_pairs={{4,8},{12,16},{20,24},{8,4},{16,12},{24,20},{5,9},{13,17},{21,25},... | collective-permute-start | bytes 786440 | tf_op jit(solution)/shard_map/ppermute | solution.py:468
  7.1 8.5 %collective-permute-start.2 = (bf16[256,256]{1,0:T(8,128)(2,1)S(1)}, bf16[256,256]{1,0:T(8,128)(2,1)S(1)}, u32[]{:S(2)}, u32[]{:S(2)}) collective-permute-start(bf16[256,256]{1,0:T(8,128)(2,1)S(1)} %get-tuple-element.30), channel_id=1, source_target_pairs={{0,1},{2,3},{1,0},{3,2},{4,5},{6,7},{5,4},{7,6},{8,9},{10,11},{9,8... | collective-permute-start | bytes 393224 | tf_op jit(solution)/shard_map/ppermute | solution.py:468
  9.7 5.8 %collective-permute-start.3 = (bf16[256,256]{1,0:T(8,128)(2,1)S(1)}, bf16[256,256]{1,0:T(8,128)(2,1)S(1)}, u32[]{:S(2)}, u32[]{:S(2)}) collective-permute-start(bf16[256,256]{1,0:T(8,128)(2,1)S(1)} %get-tuple-element.31), channel_id=1, source_target_pairs={{1,2},{2,1},{5,6},{6,5},{9,10},{10,9},{13,14},{14,13},{17,18},{18,... | collective-permute-start | bytes 393224 | tf_op jit(solution)/shard_map/ppermute | solution.py:468

commit v4 on v3

--- a/solution.py
+++ b/solution.py
@@ -60,36 +60,56 @@
     return jnp.sum(jnp.where(mask, matrix, 0.0), axis=1, keepdims=True)
 
 
-def eliminate(matrix, full):
-    size, width = matrix.shape
-    row = iota((size, width), 0)
+def eliminate(problems, beside=None):
+    matrices = [matrix for matrix, _ in problems]
+    size = matrices[0].shape[0]
+    rows = [iota(matrix.shape, 0) for matrix in matrices]
     for start in range(0, size, PANEL):
-        columns = [
-            jnp.broadcast_to(matrix[:, start + t : start + t + 1], (size, width)) for t in range(PANEL)
+        panels = [
+            [jnp.broadcast_to(matrix[:, start + t : start + t + 1], matrix.shape) for t in range(PANEL)]
+            for matrix in matrices
         ]
         for t in range(PANEL):
             at = start + t
-            factor = columns[t] * (1.0 / columns[t][at : at + 1, :])
-            factor = jnp.where(row != at if full else row > at, factor, 0.0)
-            for s in range(t + 1, PANEL):
-                columns[s] = columns[s] - factor * columns[s][at : at + 1, :]
-            matrix = matrix - factor * matrix[at : at + 1, :]
-    return matrix
-
-
-def cholesky_inverse(gram):
-    size = gram.shape[0]
-    matrix = eliminate(jnp.concatenate([gram, eye(size)], axis=1), False)
+            for which, (_, full) in enumerate(problems):
+                columns = panels[which]
+                factor = columns[t] * (1.0 / columns[t][at : at + 1, :])
+                factor = jnp.where(rows[which] != at if full else rows[which] > at, factor, 0.0)
+                for s in range(t + 1, PANEL):
+                    columns[s] = columns[s] - factor * columns[s][at : at + 1, :]
+                matrices[which] = matrices[which] - factor * matrices[which][at : at + 1, :]
+        if beside is not None:
+            beside()
+    return matrices
+
+
+def cholesky_problem(gram):
+    return jnp.concatenate([gram, eye(gram.shape[0])], axis=1), False
+
+
+def cholesky_result(matrix):
+    size = matrix.shape[0]
     upper = matrix[:, :size]
     scale = lax.rsqrt(diagonal_of(upper))
     upper = jnp.where(iota((size, size), 0) <= iota((size, size), 1), upper, 0.0)
     return upper * scale, matrix[:, size:] * scale
 
 
+def cholesky_inverse(gram, beside=None):
+    return cholesky_result(eliminate([cholesky_problem(gram)], beside)[0])
+
+
+def solve_problem(square, right):
+    return jnp.concatenate([square, right], axis=1), True
+
+
+def solve_result(matrix):
+    size = matrix.shape[0]
+    return matrix[:, size:] / diagonal_of(matrix[:, :size])
+
+
 def solve(square, right):
-    size = square.shape[0]
-    matrix = eliminate(jnp.concatenate([square, right], axis=1), True)
-    return matrix[:, size:] / diagonal_of(matrix[:, :size])
+    return solve_result(eliminate([solve_problem(square, right)])[0])
 
 
 def spread_matrix(count):
@@ -334,11 +354,11 @@
     count = inputs.shape[1] // 2
     on, on_small = eye(WINDOW), eye(count)
     root = math.sqrt(2.0)
-    moved_rows = mm(inputs, resolvent, TN)
+    moved_rows = mm_three(inputs, resolvent, TN)
     sense_row = moved_rows[count:]
-    drive_column = mm(resolvent, inputs[:, :count])
+    drive_column = mm_three(resolvent, inputs[:, :count])
     both = jnp.concatenate([inputs[:, :count].T, moved_rows[:count]], axis=0)
-    overlap = mm(inputs[:, count:], drive_column, TN)
+    overlap = mm_three(inputs[:, count:], drive_column, TN)
     first = on - 2.0 * resolvent
     beside()
     factor = lyapunov_factor(root * sense_row, first, beside)
@@ -346,15 +366,15 @@
         seen = mm(both, factor, NT)
         beside()
         small = on_small + mm(seen[count:], seen[:count], NT)
-        moved = mm(seen[:count], factor)
+        moved = mm_three(seen[:count], factor)
         normal = mm(small, small, NT)
-        moved = mm(moved, resolvent)
+        moved = mm_three(moved, resolvent)
         beside()
         beside()
-        scaled = mm(solve(normal, small), moved)
-        start = jnp.concatenate([sense_row - mm(overlap, scaled), scaled], axis=0)
-        factor = lyapunov_factor(root * start, first + 2.0 * mm(drive_column, scaled), beside)
-    return mm(factor, factor, TN)
+        scaled = mm_three(solve(normal, small), moved)
+        start = jnp.concatenate([sense_row - mm_three(overlap, scaled), scaled], axis=0)
+        factor = lyapunov_factor(root * start, first + 2.0 * mm_three(drive_column, scaled), beside)
+    return mm_three(factor, factor, TN)
 
 
 def finish_kernel(
@@ -376,21 +396,33 @@
         return totals
 
     def take_group(group, total):
+        mixed = unpack(gathered[pl.ds(group * GROUP, GROUP), :SUB], 0, WINDOW)
+        factors = jnp.where(row <= column, mixed, 0.0).T
+        wide_held[group] = factors
+        return total + mm(factors, factors, NT)
+
+    def take_image(group, carry):
         stack = gathered[pl.ds(group * GROUP, GROUP)]
         mixed = unpack(stack[:, :SUB], 0, WINDOW)
-        factors = jnp.where(row <= column, mixed, 0.0).T
         half_diagonal = 0.5 * unpack(stack[:, SUB:], 64, 1)
         image = jnp.where(row > column, mixed, jnp.where(row == column, half_diagonal, 0.0))
         for at, piece in enumerate(split(image)):
             blocks_held[group, at] = jnp.where(same_block, dot(piece, repeat), 0.0).astype(bf16)
-        wide_held[group] = factors
         inputs_held[group] = unpack(stack[:, SUB:], 0, 16)
-        return total + mm(factors, factors, NT)
+        return carry
 
     scale = 1.0 / (1.0 + SECOND_SHIFT)
     gram = scale * loop(take_group, jnp.zeros((WINDOW, WINDOW), f32))
     gram_out[...] = gram
-    _, first = cholesky_inverse(gram)
+    images_left = list(range(groups)) if groups <= 4 else []
+    if groups > 4:
+        loop(take_image, 0)
+
+    def next_image():
+        if images_left:
+            take_image(images_left.pop(0), 0)
+
+    _, first = cholesky_inverse(gram, next_image)
 
     def group_step(group, totals):
         change = mm(first, wide_held[group])
@@ -406,8 +438,9 @@
     gram_second, raw, inputs = loop(group_step, (zeros, zeros, jnp.zeros((WINDOW, 16), f32)))
     gram_second = scale * gram_second
     raw = raw + raw.T
-    upper, second = cholesky_inverse(gram_second)
-    core = solve(gram_second - raw, eye(WINDOW))
+    factored, solved = eliminate([cholesky_problem(gram_second), solve_problem(gram_second - raw, eye(WINDOW))])
+    upper, second = cholesky_result(factored)
+    core = solve_result(solved)
     resolvent = mm_three(mm_three(upper, core), upper, NT)
     inputs = mm_three(second, inputs)
     projected = mm_three(mm_three(second, raw), second, NT)

time: 57 us -> 56.3 us (0.988)
  Pallas kernels: 32.2 us -> 31.5 us
    pallas_call x1, Pallas kernels: 17.3 us -> 16.7 us  [local(): pl.pallas_call(finish_kernel, out_shape=(shape(window_shape, bf16), shape...]
where the time goes in v4:
time: 56.3 us; the launch traced here: 56.1 us
  Pallas kernels  31.5 us (56%)
  blocking collectives  18.5 us (33%)
  starting transfers between devices  4.5 us (8%)
  between operations  1.51 us (3%)
    all_to_all x1, blocking collectives, local(): gathered = lax.all_to_all(payload, ('gx', 'gy'), 0, 0)  18.5 us
    pallas_call x1, Pallas kernels, local(): pl.pallas_call(finish_kernel, out_shape=(shape(window_shape, bf16), shape...  16.7 us
    pallas_call x1, Pallas kernels, local(): pl.pallas_call(functools.partial(project_kernel, weight), out_shape=(shap...  5.23 us
    pallas_call x1, Pallas kernels, local(): pl.pallas_call(functools.partial(transform_kernel, weight), out_shape=(sh...  5.13 us
    pallas_call x1, Pallas kernels, local(): pl.pallas_call(functools.partial(frame_kernel, weight), out_shape=(shape(...  4.51 us
    ppermute x4, starting transfers between devices, exchange(): return lax.ppermute(face, axis, pairs + [(b, a) for a, b in pairs])  4.5 us
  transfers between devices with their start and end apart: 4, of which 0 were waited for; matrix products, arithmetic and copies ran while one was open for 0% of the time, Pallas kernels for 9%

profile of v4, /device:TPU:0, one launch (start us, length us, event | category | flops | bytes accessed | tf_op | source)
XLA Modules:
  0.0 56.1 jit_solution(7658684045384104748)
XLA Ops:
  1.3 0.1 pad_add_fusion.scalars
  1.4 4.5 %frame.1 = (f32[32,128]{1,0:T(8,128)S(1)}, bf16[8,2,256,256]{3,2,1,0:T(8,128)(2,1)S(1)}, bf16[32,16,256]{2,1,0:T(8,128)(2,1)S(1)}, bf16[32,16,256]{2,1,0:T(8,128...) custom-call(s32[3]{0:T(128)S(1)} %pad_add_fusion.scalars, ...), custom_call_target="tpu_custom_call" | custom-call | tf_op jit(solution)/shard_map/frame/pallas_call | solution.py:528
  5.9 0.5 collective-permute-start
  6.4 0.7 %collective-permute-start.1 = (bf16[32,16,256]{2,1,0:T(8,128)(2,1)S(1)}, bf16[32,16,256]{2,1,0:T(8,128)(2,1)S(1)}, u32[]{:S(2)}, u32[]{:S(2)}) collective-permute-start(bf16[32,16,256]{2,1,0:T(8,128)(2,1)S(1)} %get-tuple-element.29), channel_id=1, source_target_pairs={{4,8},{12,16},{20,24},{8,4},{16,12},{24,20},{5,9},{13,17},{21,25},... | collective-permute-start | bytes 786440 | tf_op jit(solution)/shard_map/ppermute | solution.py:501
  7.1 2.7 %collective-permute-start.2 = (bf16[256,256]{1,0:T(8,128)(2,1)S(1)}, bf16[256,256]{1,0:T(8,128)(2,1)S(1)}, u32[]{:S(2)}, u32[]{:S(2)}) collective-permute-start(bf16[256,256]{1,0:T(8,128)(2,1)S(1)} %get-tuple-element.30), channel_id=1, source_target_pairs={{0,1},{2,3},{1,0},{3,2},{4,5},{6,7},{5,4},{7,6},{8,9},{10,11},{9,8... | collective-permute-start | bytes 393224 | tf_op jit(solution)/shard_map/ppermute | solution.py:501
  9.7 0.7 %collective-permute-start.3 = (bf16[256,256]{1,0:T(8,128)(2,1)S(1)}, bf16[256,256]{1,0:T(8,128)(2,1)S(1)}, u32[]{:S(2)}, u32[]{:S(2)}) collective-permute-start(bf16[256,256]{1,0:T(8,128)(2,1)S(1)} %get-tuple-element.31), channel_id=1, source_target_pairs={{1,2},{2,1},{5,6},{6,5},{9,10},{10,9},{13,14},{14,13},{17,18},{18,... | collective-permute-start | bytes 393224 | tf_op jit(solution)/shard_map/ppermute | solution.py:501
  10.4 5.1 %transform.1 = (bf16[2,256,256]{2,1,0:T(8,128)(2,1)S(1)}, f32[8,2,256,256]{3,2,1,0:T(8,128)S(1)}, bf16[8,2,2,256,256]{4,3,2,1,0:T(8,128)(2,1)S(1)}, f32[32,128]{1,0:T(8,128)S(1)}) custom-call(f32[32,128]{1,0:T(8,128)S(1)} %get-tuple-element.19.small, bf16[8,2,256,256]{3,2,1,0:T(8,128)(2,1)S(1)} %get-tuple-element.20.blocks, ...), custom_call_target="tpu_custom_call" | custom-call | flops 2000000000 | bytes 8388608 | tf_op jit(solution)/shard_map/transform/pallas_call | solution.py:556
  15.5 0.0 collective-permute-done.2.y_even
  15.5 0.0 collective-permute-done.3.y_odd
  15.6 0.0 collective-permute-done.x_even
  15.6 0.0 collective-permute-done.1.x_odd
  15.6 5.2 %project.1 = (f32[32,16,128]{2,1,0:T(8,128)S(1)}, bf16[8,2,2,256,256]{4,3,2,1,0:T(8,128)(2,1)S(1)}) custom-call(s32[3]{0:T(128)S(1)} %pad_add_fusion.scalars, bf16[2,256,256]{2,1,0:T(8,128)(2,1)S(1)} %get-tuple-element.24.frame, f32[8,2,256,256]{3,2,1,0:T(8,128)S(1)} %get-tuple-element.25.rows_all, ...), custom_call_target="tpu_custom_call" | custom-call | tf_op jit(solution)/shard_map/project/pallas_call | solution.py:575
  20.8 18.5 %all_to_all.5.gathered = f32[32,16,128]{2,1,0:T(8,128)S(1)} all-to-all(f32[32,16,128]{2,1,0:T(8,128)S(1)} %get-tuple-element.32), channel_id=1, replica_groups=mesh['gx'=8,'gy'=4] {'gx','gy'}, dimensions={0} | all-to-all | bytes 524288 | tf_op jit(solution)/shard_map/all_to_all | solution.py:590
  39.3 16.7 %finish.1 = (bf16[32,8,16,256]{3,2,1,0:T(8,128)(2,1)}, bf16[32,8,16,256]{3,2,1,0:T(8,128)(2,1)}, f32[32,32]{1,0:T(8,128)}, f32[32,32]{1,0:T(8,128)}) custom-call(f32[32,128]{1,0:T(8,128)S(1)} %get-tuple-element.23.products, f32[32,16,128]{2,1,0:T(8,128)S(1)} %all_to_all.5.gathered, bf16[8,2,2,256,256]{4,3,2,1,0:T(8,128)(2,1)S(1)} %get-tuple-element.26.fields, ...), custom_call_target="tpu_custom_call" | custom-call | tf_op jit(solution)/shard_map/finish/pallas_call | solution.py:591
Async XLA Ops:
  5.9 9.7 %collective-permute-start = (bf16[32,16,256]{2,1,0:T(8,128)(2,1)S(1)}, bf16[32,16,256]{2,1,0:T(8,128)(2,1)S(1)}, u32[]{:S(2)}, u32[]{:S(2)}) collective-permute-start(bf16[32,16,256]{2,1,0:T(8,128)(2,1)S(1)} %get-tuple-element.28), channel_id=1, source_target_pairs={{0,4},{8,12},{16,20},{24,28},{4,0},{12,8},{20,16},{28,24},{1,5},{9... | collective-permute-start | bytes 786440 | tf_op jit(solution)/shard_map/ppermute | solution.py:501
  6.4 9.2 %collective-permute-start.1 = (bf16[32,16,256]{2,1,0:T(8,128)(2,1)S(1)}, bf16[32,16,256]{2,1,0:T(8,128)(2,1)S(1)}, u32[]{:S(2)}, u32[]{:S(2)}) collective-permute-start(bf16[32,16,256]{2,1,0:T(8,128)(2,1)S(1)} %get-tuple-element.29), channel_id=1, source_target_pairs={{4,8},{12,16},{20,24},{8,4},{16,12},{24,20},{5,9},{13,17},{21,25},... | collective-permute-start | bytes 786440 | tf_op jit(solution)/shard_map/ppermute | solution.py:501
  7.1 8.5 %collective-permute-start.2 = (bf16[256,256]{1,0:T(8,128)(2,1)S(1)}, bf16[256,256]{1,0:T(8,128)(2,1)S(1)}, u32[]{:S(2)}, u32[]{:S(2)}) collective-permute-start(bf16[256,256]{1,0:T(8,128)(2,1)S(1)} %get-tuple-element.30), channel_id=1, source_target_pairs={{0,1},{2,3},{1,0},{3,2},{4,5},{6,7},{5,4},{7,6},{8,9},{10,11},{9,8... | collective-permute-start | bytes 393224 | tf_op jit(solution)/shard_map/ppermute | solution.py:501
  9.7 5.8 %collective-permute-start.3 = (bf16[256,256]{1,0:T(8,128)(2,1)S(1)}, bf16[256,256]{1,0:T(8,128)(2,1)S(1)}, u32[]{:S(2)}, u32[]{:S(2)}) collective-permute-start(bf16[256,256]{1,0:T(8,128)(2,1)S(1)} %get-tuple-element.31), channel_id=1, source_target_pairs={{1,2},{2,1},{5,6},{6,5},{9,10},{10,9},{13,14},{14,13},{17,18},{18,... | collective-permute-start | bytes 393224 | tf_op jit(solution)/shard_map/ppermute | solution.py:501

commit v5 on v4

--- a/solution.py
+++ b/solution.py
@@ -144,43 +144,30 @@
     return part.reshape(rows.shape[0] * SUB, rows.shape[2]).astype(bf16)
 
 
-def frame_kernel(
-    weight, scalars, factor, actuators, sensors, diagonal,
-    small, blocks, x_even, x_odd, y_even, y_odd, act_held, sens_held, coefficient, window, total, sems, other_sems,
+def face_kernel(
+    scalars, factor, blocks, x_even, x_odd, y_even, y_odd, window, sems,
 ):
     planes, rows, depth = window.shape[1:]
-    step = 2
+    step = 1
     copies = [
         pltpu.make_async_copy(
             factor.at[pl.ds(scalars[0], WINDOW), pl.ds(x, step)], window.at[:, pl.ds(x, step)], sems.at[x // step]
         )
         for x in range(0, planes, step)
     ]
-    others = [
-        pltpu.make_async_copy(actuators, act_held, other_sems.at[0]),
-        pltpu.make_async_copy(sensors, sens_held, other_sems.at[1]),
-        pltpu.make_async_copy(diagonal, coefficient, other_sems.at[2]),
-    ]
-    for copy in copies + others:
+    for copy in copies:
         copy.start()
     sub = iota((WINDOW, planes, depth), 1)
     low_y = jnp.zeros((WINDOW, planes, depth), f32)
     high_y = jnp.zeros((WINDOW, planes, depth), f32)
     for start in range(0, planes, step):
         copies[start // step].wait()
-        parts = []
         for x in range(start, start + step):
             plane = window[:, x].astype(f32)
             for half in range(rows // SUB):
-                parts.append(block(plane, half))
-                blocks[x, half] = parts[-1]
+                blocks[x, half] = block(plane, half)
             low_y = jnp.where(sub == x, jnp.broadcast_to(plane[:, :1], low_y.shape), low_y)
             high_y = jnp.where(sub == x, jnp.broadcast_to(plane[:, rows - 1 :], high_y.shape), high_y)
-        parts = jnp.concatenate(parts, axis=1)
-        if start == 0:
-            total[...] = dot(parts, parts, NT)
-        else:
-            total[...] += dot(parts, parts, NT)
     x_first = scalars[1] == 0
     y_first = scalars[2] == 0
     first, last = window[:, 0], window[:, planes - 1]
@@ -190,12 +177,6 @@
     high_y = high_y.reshape(WINDOW * planes, depth).astype(bf16)
     y_even[...] = jnp.where(y_first, high_y, low_y)
     y_odd[...] = jnp.where(y_first, low_y, high_y)
-    gram = reduce_rows(total[...]) * weight
-    on = eye(WINDOW)
-    upper, inverse = cholesky_inverse(gram + on * (SHIFT * gram + FLOOR))
-    small[...] = jnp.concatenate([upper, inverse, jnp.zeros((WINDOW, 64), f32)], axis=1)
-    for copy in others:
-        copy.wait()
 
 
 def transform(frame, rows_here):
@@ -203,19 +184,53 @@
 
 
 def transform_kernel(
-    weight, small, blocks, actuators, sensors, frame, rows_all, fields, products, gram_a, gram_b, input_a,
+    weight, blocks, actuators_hbm, sensors_hbm, diagonal, frame, rows_all, fields, products, coefficient,
+    actuators, sensors, gram_a, gram_b, input_a, sems,
 ):
     planes, halves = blocks.shape[:2]
-    upper = small[:, :WINDOW]
-    pieces = split(small[:, WINDOW : 2 * WINDOW])
+    gram_a[...] = jnp.zeros_like(gram_a)
+    gram_b[...] = jnp.zeros_like(gram_b)
+    input_a[...] = jnp.zeros_like(input_a)
+
+    copies = [
+        pltpu.make_async_copy(actuators_hbm, actuators, sems.at[0]),
+        pltpu.make_async_copy(sensors_hbm, sensors, sems.at[1]),
+        pltpu.make_async_copy(diagonal, coefficient, sems.at[2]),
+    ]
+    for copy in copies:
+        copy.start()
+
+    def window_step(x):
+        rows_here = jnp.concatenate([blocks[x, half] for half in range(halves)], axis=1)
+        gram_a[...] += dot(rows_here, rows_here, NT)
+
+    def input_step(x):
+        act_plane, sens_plane = actuators[:, x].astype(f32), sensors[:, x].astype(f32)
+        inputs = [
+            jnp.concatenate([block(act_plane, half), block(sens_plane, half)], axis=0) for half in range(halves)
+        ]
+        rows_here = jnp.concatenate([blocks[x, half] for half in range(halves)], axis=1)
+        input_a[...] += dot(rows_here, jnp.concatenate(inputs, axis=1), NT)
+
+    for x in range(planes):
+        window_step(x)
+    gram = reduce_rows(gram_a[...]) * weight
+    gram_a[...] = jnp.zeros_like(gram_a)
+    waiting = list(range(planes))
+    for copy in copies:
+        copy.wait()
+
+    def next_inputs():
+        for x in waiting[: planes * PANEL // WINDOW]:
+            input_step(x)
+        del waiting[: planes * PANEL // WINDOW]
+
+    on = eye(WINDOW)
+    upper, inverse = cholesky_inverse(gram + on * (SHIFT * gram + FLOOR), next_inputs)
+    pieces = split(inverse)
     for at, piece in enumerate(expand(pieces)):
         frame[at] = piece
     rounded = pieces[0].astype(f32) + pieces[1].astype(f32)
-    for _ in range(2):
-        upper = upper - mm(mm(upper, rounded, NT) - eye(WINDOW), upper)
-    gram_a[...] = jnp.zeros_like(gram_a)
-    gram_b[...] = jnp.zeros_like(gram_b)
-    input_a[...] = jnp.zeros_like(input_a)
 
     def plane_step(x):
         for half in range(halves):
@@ -231,24 +246,25 @@
         gram_a[...] += dot(highs, highs, NT)
         gram_b[...] += dot(highs, lows, NT)
 
-    def input_step(x):
-        act_plane, sens_plane = actuators[:, x].astype(f32), sensors[:, x].astype(f32)
-        inputs = [
-            jnp.concatenate([block(act_plane, half), block(sens_plane, half)], axis=0) for half in range(halves)
-        ]
-        rows_here = jnp.concatenate([blocks[x, half] for half in range(halves)], axis=1)
-        input_a[...] += dot(rows_here, jnp.concatenate(inputs, axis=1), NT)
-
     for x in range(planes + 1):
         if x < planes:
             plane_step(x)
-            input_step(x)
         if x > 0:
             gram_step(x - 1)
     cross = reduce_rows(gram_b[...])
     gram = (reduce_rows(gram_a[...]) + cross + cross.T) * weight
-    second_upper, second = cholesky_inverse(gram + SECOND_SHIFT * eye(WINDOW))
-    inputs = mm(second, mm(rounded, reduce_rows(input_a[...]) * weight))
+    inputs = mm(rounded, reduce_rows(input_a[...]) * weight)
+    state = [upper]
+
+    def newton():
+        if len(state) == 1:
+            state.append(mm(state[0], rounded, NT) - on)
+        else:
+            state[:] = [state[0] - mm(state[1], state[0])]
+
+    second_upper, second = cholesky_inverse(gram + SECOND_SHIFT * on, newton)
+    upper = state[0]
+    inputs = mm(second, inputs)
     products[...] = jnp.concatenate(
         [mm(second_upper, upper), second, upper, inputs, jnp.zeros((WINDOW, 16), f32)], axis=1
     )
@@ -525,53 +541,51 @@
     )
     pair_shape = (planes, halves, 2, ROWS, depth)
     rows_shape = (planes, halves, ROWS, depth)
-    small, blocks, x_even, x_odd, y_even, y_odd, act_held, sens_held, coefficient = pl.pallas_call(
-        functools.partial(frame_kernel, weight),
+    blocks, x_even, x_odd, y_even, y_odd = pl.pallas_call(
+        face_kernel,
         out_shape=(
-            shape((WINDOW, 128), f32),
             shape(rows_shape, bf16),
             x_face,
             x_face,
             y_face,
             y_face,
-            shape(actuators.shape, bf16),
-            shape(sensors.shape, bf16),
-            shape(diagonal.shape, f32),
         ),
-        in_specs=[smem] + [hbm] * 4,
-        out_specs=(vmem,) * 9,
+        in_specs=[smem, hbm],
+        out_specs=(vmem,) * 5,
         scratch_shapes=[
             pltpu.VMEM(window_shape, bf16),
-            pltpu.VMEM((ROWS, ROWS), f32),
             pltpu.SemaphoreType.DMA((planes,)),
-            pltpu.SemaphoreType.DMA((3,)),
         ],
         compiler_params=params(16),
-        name="frame",
-    )(scalars, factor, actuators, sensors, diagonal)
+        name="faces",
+    )(scalars, factor)
     x_even = exchange(x_even, "gx", False)
     x_odd = exchange(x_odd, "gx", True)
     y_even = exchange(y_even, "gy", False)
     y_odd = exchange(y_odd, "gy", True)
-    frame, rows_all, fields, products = pl.pallas_call(
+    frame, rows_all, fields, products, coefficient = pl.pallas_call(
         functools.partial(transform_kernel, weight),
         out_shape=(
             shape((2, ROWS, ROWS), bf16),
             shape(rows_shape, f32),
             shape(pair_shape, bf16),
             shape((WINDOW, 128), f32),
+            shape(diagonal.shape, f32),
         ),
-        in_specs=[vmem] * 4,
-        out_specs=(vmem,) * 4,
+        in_specs=[vmem] + [hbm] * 3,
+        out_specs=(vmem,) * 5,
         scratch_shapes=[
+            pltpu.VMEM(actuators.shape, bf16),
+            pltpu.VMEM(sensors.shape, bf16),
             pltpu.VMEM((ROWS, ROWS), f32),
             pltpu.VMEM((ROWS, ROWS), f32),
             pltpu.VMEM((ROWS, 16 * SUB), f32),
+            pltpu.SemaphoreType.DMA((3,)),
         ],
         compiler_params=params(16),
         cost_estimate=pl.CostEstimate(flops=2 * 10**9, bytes_accessed=8 * 2**20, transcendentals=0),
         name="transform",
-    )(small, blocks, act_held, sens_held)
+    )(blocks, actuators, sensors, diagonal)
     payload, images = pl.pallas_call(
         functools.partial(project_kernel, weight),
         out_shape=(shape((devices, 2 * SUB, 128), f32), shape(pair_shape, bf16)),

time: 56.3 us -> 55.6 us (0.988)
  Pallas kernels: 31.5 us -> 30.8 us
    pallas_call x1, Pallas kernels: 4.51 us -> 2.29 us  [local(): pl.pallas_call(face_kernel, out_shape=(shape(rows_shape, bf16), x_face, x...]
    pallas_call x1, Pallas kernels: 5.13 us -> 6.6 us  [local(): pl.pallas_call(functools.partial(transform_kernel, weight), out_shape=(sh...]
  transfers between devices with their start and end apart: 4 -> 4, of which waited for: 0 -> 0; matrix products, arithmetic and copies ran while one was open for 0% -> 0% of each run, Pallas kernels for 9% -> 12%
where the time goes in v5:
time: 55.6 us; the launch traced here: 55.4 us
  Pallas kernels  30.8 us (55%)
  blocking collectives  18.5 us (33%)
  starting transfers between devices  4.5 us (8%)
  between operations  1.53 us (3%)
    all_to_all x1, blocking collectives, local(): gathered = lax.all_to_all(payload, ('gx', 'gy'), 0, 0)  18.5 us
    pallas_call x1, Pallas kernels, local(): pl.pallas_call(finish_kernel, out_shape=(shape(window_shape, bf16), shape...  16.7 us
    pallas_call x1, Pallas kernels, local(): pl.pallas_call(functools.partial(transform_kernel, weight), out_shape=(sh...  6.6 us
    pallas_call x1, Pallas kernels, local(): pl.pallas_call(functools.partial(project_kernel, weight), out_shape=(shap...  5.24 us
    ppermute x4, starting transfers between devices, exchange(): return lax.ppermute(face, axis, pairs + [(b, a) for a, b in pairs])  4.5 us
    pallas_call x1, Pallas kernels, local(): pl.pallas_call(face_kernel, out_shape=(shape(rows_shape, bf16), x_face, x...  2.29 us
  transfers between devices with their start and end apart: 4, of which 0 were waited for; matrix products, arithmetic and copies ran while one was open for 0% of the time, Pallas kernels for 12%

profile of v5, /device:TPU:0, one launch (start us, length us, event | category | flops | bytes accessed | tf_op | source)
XLA Modules:
  0.0 55.4 jit_solution(6967823729080506513)
XLA Ops:
  1.3 0.1 pad_add_fusion.scalars
  1.4 2.3 %faces.1 = (bf16[8,2,256,256]{3,2,1,0:T(8,128)(2,1)S(1)}, bf16[32,16,256]{2,1,0:T(8,128)(2,1)S(1)}, bf16[32,16,256]{2,1,0:T(8,128)(2,1)S(1)}, bf16[256,256]{1,0:T(8,128)(2,1)S(1)}, bf16[256,256]{1,0:T(8,128)(2,1)S(1)}) custom-call(s32[3]{0:T(128)S(1)} %pad_add_fusion.scalars, bf16[64,8,16,256]{3,2,1,0:T(8,128)(2,1)} %factor.1), custom_call_target="tpu_custom_call" | custom-call | tf_op jit(solution)/shard_map/faces/pallas_call | solution.py:544
  3.7 0.5 collective-permute-start
  4.2 0.7 %collective-permute-start.1 = (bf16[32,16,256]{2,1,0:T(8,128)(2,1)S(1)}, bf16[32,16,256]{2,1,0:T(8,128)(2,1)S(1)}, u32[]{:S(2)}, u32[]{:S(2)}) collective-permute-start(bf16[32,16,256]{2,1,0:T(8,128)(2,1)S(1)} %get-tuple-element.23), channel_id=1, source_target_pairs={{4,8},{12,16},{20,24},{8,4},{16,12},{24,20},{5,9},{13,17},{21,25},... | collective-permute-start | bytes 786440 | tf_op jit(solution)/shard_map/ppermute | solution.py:517
  4.9 2.7 %collective-permute-start.2 = (bf16[256,256]{1,0:T(8,128)(2,1)S(1)}, bf16[256,256]{1,0:T(8,128)(2,1)S(1)}, u32[]{:S(2)}, u32[]{:S(2)}) collective-permute-start(bf16[256,256]{1,0:T(8,128)(2,1)S(1)} %get-tuple-element.24), channel_id=1, source_target_pairs={{0,1},{2,3},{1,0},{3,2},{4,5},{6,7},{5,4},{7,6},{8,9},{10,11},{9,8... | collective-permute-start | bytes 393224 | tf_op jit(solution)/shard_map/ppermute | solution.py:517
  7.5 0.7 %collective-permute-start.3 = (bf16[256,256]{1,0:T(8,128)(2,1)S(1)}, bf16[256,256]{1,0:T(8,128)(2,1)S(1)}, u32[]{:S(2)}, u32[]{:S(2)}) collective-permute-start(bf16[256,256]{1,0:T(8,128)(2,1)S(1)} %get-tuple-element.25), channel_id=1, source_target_pairs={{1,2},{2,1},{5,6},{6,5},{9,10},{10,9},{13,14},{14,13},{17,18},{18,... | collective-permute-start | bytes 393224 | tf_op jit(solution)/shard_map/ppermute | solution.py:517
  8.2 6.6 %transform.1 = (bf16[2,256,256]{2,1,0:T(8,128)(2,1)S(1)}, f32[8,2,256,256]{3,2,1,0:T(8,128)S(1)}, bf16[8,2,2,256,256]{4,3,2,1,0:T(8,128)(2,1)S(1)}, f32[32,128]{1,0:T(8,128)S(1)}, f32[8,16,256]{2,1,0:T(8,128)S(1)}) custom-call(bf16[8,2,256,256]{3,2,1,0:T(8,128)(2,1)S(1)} %get-tuple-element.16.blocks, bf16[8,8,16,256]{3,2,1,0:T(8,128)(2,1)} %actuators_hbm.1, ...), custom_call_target="tpu_custom_call" | custom-call | flops 2000000000 | bytes 8388608 | tf_op jit(solution)/shard_map/transform/pallas_call | solution.py:566
  14.8 0.0 collective-permute-done.2.y_even
  14.8 0.0 collective-permute-done.3.y_odd
  14.8 0.0 collective-permute-done.x_even
  14.8 0.0 collective-permute-done.1.x_odd
  14.8 5.2 %project.1 = (f32[32,16,128]{2,1,0:T(8,128)S(1)}, bf16[8,2,2,256,256]{4,3,2,1,0:T(8,128)(2,1)S(1)}) custom-call(s32[3]{0:T(128)S(1)} %pad_add_fusion.scalars, bf16[2,256,256]{2,1,0:T(8,128)(2,1)S(1)} %get-tuple-element.18.frame, f32[8,2,256,256]{3,2,1,0:T(8,128)S(1)} %get-tuple-element.19.rows_all, ...), custom_call_target="tpu_custom_call" | custom-call | tf_op jit(solution)/shard_map/project/pallas_call | solution.py:589
  20.1 18.5 %all_to_all.5.gathered = f32[32,16,128]{2,1,0:T(8,128)S(1)} all-to-all(f32[32,16,128]{2,1,0:T(8,128)S(1)} %get-tuple-element.26), channel_id=1, replica_groups=mesh['gx'=8,'gy'=4] {'gx','gy'}, dimensions={0} | all-to-all | bytes 524288 | tf_op jit(solution)/shard_map/all_to_all | solution.py:604
  38.6 16.7 %finish.1 = (bf16[32,8,16,256]{3,2,1,0:T(8,128)(2,1)}, bf16[32,8,16,256]{3,2,1,0:T(8,128)(2,1)}, f32[32,32]{1,0:T(8,128)}, f32[32,32]{1,0:T(8,128)}) custom-call(f32[32,128]{1,0:T(8,128)S(1)} %get-tuple-element.17.products, f32[32,16,128]{2,1,0:T(8,128)S(1)} %all_to_all.5.gathered, bf16[8,2,2,256,256]{4,3,2,1,0:T(8,128)(2,1)S(1)} %get-tuple-element.20.fields, ...), custom_call_target="tpu_custom_call" | custom-call | tf_op jit(solution)/shard_map/finish/pallas_call | solution.py:605
Async XLA Ops:
  3.7 11.1 %collective-permute-start = (bf16[32,16,256]{2,1,0:T(8,128)(2,1)S(1)}, bf16[32,16,256]{2,1,0:T(8,128)(2,1)S(1)}, u32[]{:S(2)}, u32[]{:S(2)}) collective-permute-start(bf16[32,16,256]{2,1,0:T(8,128)(2,1)S(1)} %get-tuple-element.22), channel_id=1, source_target_pairs={{0,4},{8,12},{16,20},{24,28},{4,0},{12,8},{20,16},{28,24},{1,5},{9... | collective-permute-start | bytes 786440 | tf_op jit(solution)/shard_map/ppermute | solution.py:517
  4.2 10.6 %collective-permute-start.1 = (bf16[32,16,256]{2,1,0:T(8,128)(2,1)S(1)}, bf16[32,16,256]{2,1,0:T(8,128)(2,1)S(1)}, u32[]{:S(2)}, u32[]{:S(2)}) collective-permute-start(bf16[32,16,256]{2,1,0:T(8,128)(2,1)S(1)} %get-tuple-element.23), channel_id=1, source_target_pairs={{4,8},{12,16},{20,24},{8,4},{16,12},{24,20},{5,9},{13,17},{21,25},... | collective-permute-start | bytes 786440 | tf_op jit(solution)/shard_map/ppermute | solution.py:517
  4.9 9.9 %collective-permute-start.2 = (bf16[256,256]{1,0:T(8,128)(2,1)S(1)}, bf16[256,256]{1,0:T(8,128)(2,1)S(1)}, u32[]{:S(2)}, u32[]{:S(2)}) collective-permute-start(bf16[256,256]{1,0:T(8,128)(2,1)S(1)} %get-tuple-element.24), channel_id=1, source_target_pairs={{0,1},{2,3},{1,0},{3,2},{4,5},{6,7},{5,4},{7,6},{8,9},{10,11},{9,8... | collective-permute-start | bytes 393224 | tf_op jit(solution)/shard_map/ppermute | solution.py:517
  7.5 7.3 %collective-permute-start.3 = (bf16[256,256]{1,0:T(8,128)(2,1)S(1)}, bf16[256,256]{1,0:T(8,128)(2,1)S(1)}, u32[]{:S(2)}, u32[]{:S(2)}) collective-permute-start(bf16[256,256]{1,0:T(8,128)(2,1)S(1)} %get-tuple-element.25), channel_id=1, source_target_pairs={{1,2},{2,1},{5,6},{6,5},{9,10},{10,9},{13,14},{14,13},{17,18},{18,... | collective-permute-start | bytes 393224 | tf_op jit(solution)/shard_map/ppermute | solution.py:517

commit v6 on v5

--- a/solution.py
+++ b/solution.py
@@ -471,43 +471,51 @@
         x, half = tasks.pop(0)
         field_high, field_low = fields[x, half, 0], fields[x, half, 1]
         image_high, image_low = images[x, half, 0], images[x, half, 1]
-        basis = dot(change_high, field_high) + dot(change_low, field_high) + dot(change_high, field_low)
         rest = dot(change_high, image_high) + dot(change_low, image_high) + dot(change_high, image_low)
         rest = rest + (dot(remove_high, field_high) + dot(remove_low, field_high) + dot(remove_high, field_low))
-        for at, piece in enumerate(split(basis) + split(rest)):
+        for at, piece in enumerate(split(rest)):
             prepared[x, half, at] = piece
 
     riccati = riccati_solve(resolvent, inputs, prepare)
     riccati_out[...] = riccati
     while tasks:
         prepare()
-    rotate_high, rotate_low = expand(split(riccati))
-
-    def out_copies(x):
-        return (
-            pltpu.make_async_copy(rotated_held.at[:, pl.ds(x, 1)], rotated.at[:, pl.ds(x, 1)], out_sems.at[0, x]),
-            pltpu.make_async_copy(residual_held.at[:, pl.ds(x, 1)], residual.at[:, pl.ds(x, 1)], out_sems.at[1, x]),
-        )
-
-    def plane_step(x, carry):
-        turned, left = [], []
+    solution_high, solution_low = expand(split(riccati))
+
+    def out_copy(held, out, which, x):
+        return pltpu.make_async_copy(held.at[:, pl.ds(x, 1)], out.at[:, pl.ds(x, 1)], out_sems.at[which, x])
+
+    def write(held, out, which, x, parts):
+        parts = [part.reshape(WINDOW, SUB, part.shape[1]) for part in parts]
+        held[:, x] = jnp.concatenate(parts, axis=1).astype(bf16)
+        out_copy(held, out, which, x).start()
+
+    def residual_step(x):
+        parts = []
         for half in range(halves):
-            basis_high, basis_low, rest_high, rest_low = (prepared[x, half, at] for at in range(4))
-            depth = basis_high.shape[1]
-            here = dot(rotate_high, basis_high) + dot(rotate_low, basis_high) + dot(rotate_high, basis_low)
-            rest = dot(rotate_high, rest_high) + dot(rotate_low, rest_high) + dot(rotate_high, rest_low)
-            turned.append(here.reshape(WINDOW, SUB, depth))
-            left.append(rest.reshape(WINDOW, SUB, depth))
-        rotated_held[:, x] = jnp.concatenate(turned, axis=1).astype(bf16)
-        residual_held[:, x] = jnp.concatenate(left, axis=1).astype(bf16)
-        for copy in out_copies(x):
-            copy.start()
-        return carry
-
-    lax.fori_loop(0, planes, plane_step, 0, unroll=True)
+            high, low = prepared[x, half, 0], prepared[x, half, 1]
+            parts.append(dot(solution_high, high) + dot(solution_low, high) + dot(solution_high, low))
+        write(residual_held, residual, 1, x, parts)
+
+    def rotated_step(x):
+        parts = []
+        for half in range(halves):
+            high, low = fields[x, half, 0], fields[x, half, 1]
+            parts.append(dot(rotate_high, high) + dot(rotate_low, high) + dot(rotate_high, low))
+        write(rotated_held, rotated, 0, x, parts)
+
+    residual_step(0)
+    rotate = mm_three(riccati, change)
+    residual_step(1)
+    rotate_high, rotate_low = expand(split(rotate))
+    residual_step(2)
     for x in range(planes):
-        for copy in out_copies(x):
-            copy.wait()
+        rotated_step(x)
+        if x + 3 < planes:
+            residual_step(x + 3)
+    for x in range(planes):
+        out_copy(rotated_held, rotated, 0, x).wait()
+        out_copy(residual_held, residual, 1, x).wait()
 
 
 def exchange(face, axis, odd):
@@ -616,7 +624,7 @@
             pltpu.VMEM((devices // GROUP, WINDOW, GROUP * WINDOW), f32),
             pltpu.VMEM((devices // GROUP, 2, GROUP * WINDOW, GROUP * WINDOW), bf16),
             pltpu.VMEM((devices // GROUP, GROUP * WINDOW, 16), f32),
-            pltpu.VMEM((planes, halves, 4, ROWS, depth), bf16),
+            pltpu.VMEM((planes, halves, 2, ROWS, depth), bf16),
             pltpu.VMEM(window_shape, bf16),
             pltpu.VMEM(window_shape, bf16),
             pltpu.SemaphoreType.DMA((2, planes)),

time: 55.6 us -> 54.5 us (0.980)
  Pallas kernels: 30.8 us -> 29.7 us
    pallas_call x1, Pallas kernels: 16.7 us -> 15.5 us  [local(): pl.pallas_call(finish_kernel, out_shape=(shape(window_shape, bf16), shape...]
where the time goes in v6:
time: 54.5 us; the launch traced here: 54.3 us
  Pallas kernels  29.7 us (54%)
  blocking collectives  18.5 us (34%)
  starting transfers between devices  4.5 us (8%)
  between operations  1.53 us (3%)
    all_to_all x1, blocking collectives, local(): gathered = lax.all_to_all(payload, ('gx', 'gy'), 0, 0)  18.5 us
    pallas_call x1, Pallas kernels, local(): pl.pallas_call(finish_kernel, out_shape=(shape(window_shape, bf16), shape...  15.5 us
    pallas_call x1, Pallas kernels, local(): pl.pallas_call(functools.partial(transform_kernel, weight), out_shape=(sh...  6.6 us
    pallas_call x1, Pallas kernels, local(): pl.pallas_call(functools.partial(project_kernel, weight), out_shape=(shap...  5.24 us
    ppermute x4, starting transfers between devices, exchange(): return lax.ppermute(face, axis, pairs + [(b, a) for a, b in pairs])  4.5 us
    pallas_call x1, Pallas kernels, local(): pl.pallas_call(face_kernel, out_shape=(shape(rows_shape, bf16), x_face, x...  2.29 us
  transfers between devices with their start and end apart: 4, of which 0 were waited for; matrix products, arithmetic and copies ran while one was open for 0% of the time, Pallas kernels for 12%

profile of v6, /device:TPU:0, one launch (start us, length us, event | category | flops | bytes accessed | tf_op | source)
XLA Modules:
  0.0 54.3 jit_solution(5817200780771808675)
XLA Ops:
  1.3 0.1 pad_add_fusion.scalars
  1.4 2.3 %faces.1 = (bf16[8,2,256,256]{3,2,1,0:T(8,128)(2,1)S(1)}, bf16[32,16,256]{2,1,0:T(8,128)(2,1)S(1)}, bf16[32,16,256]{2,1,0:T(8,128)(2,1)S(1)}, bf16[256,256]{1,0:T(8,128)(2,1)S(1)}, bf16[256,256]{1,0:T(8,128)(2,1)S(1)}) custom-call(s32[3]{0:T(128)S(1)} %pad_add_fusion.scalars, bf16[64,8,16,256]{3,2,1,0:T(8,128)(2,1)} %factor.1), custom_call_target="tpu_custom_call" | custom-call | tf_op jit(solution)/shard_map/faces/pallas_call | solution.py:552
  3.7 0.5 collective-permute-start
  4.2 0.7 %collective-permute-start.1 = (bf16[32,16,256]{2,1,0:T(8,128)(2,1)S(1)}, bf16[32,16,256]{2,1,0:T(8,128)(2,1)S(1)}, u32[]{:S(2)}, u32[]{:S(2)}) collective-permute-start(bf16[32,16,256]{2,1,0:T(8,128)(2,1)S(1)} %get-tuple-element.23), channel_id=1, source_target_pairs={{4,8},{12,16},{20,24},{8,4},{16,12},{24,20},{5,9},{13,17},{21,25},... | collective-permute-start | bytes 786440 | tf_op jit(solution)/shard_map/ppermute | solution.py:525
  4.9 2.7 %collective-permute-start.2 = (bf16[256,256]{1,0:T(8,128)(2,1)S(1)}, bf16[256,256]{1,0:T(8,128)(2,1)S(1)}, u32[]{:S(2)}, u32[]{:S(2)}) collective-permute-start(bf16[256,256]{1,0:T(8,128)(2,1)S(1)} %get-tuple-element.24), channel_id=1, source_target_pairs={{0,1},{2,3},{1,0},{3,2},{4,5},{6,7},{5,4},{7,6},{8,9},{10,11},{9,8... | collective-permute-start | bytes 393224 | tf_op jit(solution)/shard_map/ppermute | solution.py:525
  7.5 0.7 %collective-permute-start.3 = (bf16[256,256]{1,0:T(8,128)(2,1)S(1)}, bf16[256,256]{1,0:T(8,128)(2,1)S(1)}, u32[]{:S(2)}, u32[]{:S(2)}) collective-permute-start(bf16[256,256]{1,0:T(8,128)(2,1)S(1)} %get-tuple-element.25), channel_id=1, source_target_pairs={{1,2},{2,1},{5,6},{6,5},{9,10},{10,9},{13,14},{14,13},{17,18},{18,... | collective-permute-start | bytes 393224 | tf_op jit(solution)/shard_map/ppermute | solution.py:525
  8.2 6.6 %transform.1 = (bf16[2,256,256]{2,1,0:T(8,128)(2,1)S(1)}, f32[8,2,256,256]{3,2,1,0:T(8,128)S(1)}, bf16[8,2,2,256,256]{4,3,2,1,0:T(8,128)(2,1)S(1)}, f32[32,128]{1,0:T(8,128)S(1)}, f32[8,16,256]{2,1,0:T(8,128)S(1)}) custom-call(bf16[8,2,256,256]{3,2,1,0:T(8,128)(2,1)S(1)} %get-tuple-element.16.blocks, bf16[8,8,16,256]{3,2,1,0:T(8,128)(2,1)} %actuators_hbm.1, ...), custom_call_target="tpu_custom_call" | custom-call | flops 2000000000 | bytes 8388608 | tf_op jit(solution)/shard_map/transform/pallas_call | solution.py:574
  14.8 0.0 collective-permute-done.2.y_even
  14.8 0.0 collective-permute-done.3.y_odd
  14.8 0.0 collective-permute-done.x_even
  14.8 0.0 collective-permute-done.1.x_odd
  14.8 5.2 %project.1 = (f32[32,16,128]{2,1,0:T(8,128)S(1)}, bf16[8,2,2,256,256]{4,3,2,1,0:T(8,128)(2,1)S(1)}) custom-call(s32[3]{0:T(128)S(1)} %pad_add_fusion.scalars, bf16[2,256,256]{2,1,0:T(8,128)(2,1)S(1)} %get-tuple-element.18.frame, f32[8,2,256,256]{3,2,1,0:T(8,128)S(1)} %get-tuple-element.19.rows_all, ...), custom_call_target="tpu_custom_call" | custom-call | tf_op jit(solution)/shard_map/project/pallas_call | solution.py:597
  20.1 18.5 %all_to_all.5.gathered = f32[32,16,128]{2,1,0:T(8,128)S(1)} all-to-all(f32[32,16,128]{2,1,0:T(8,128)S(1)} %get-tuple-element.26), channel_id=1, replica_groups=mesh['gx'=8,'gy'=4] {'gx','gy'}, dimensions={0} | all-to-all | bytes 524288 | tf_op jit(solution)/shard_map/all_to_all | solution.py:612
  38.6 15.5 %finish.1 = (bf16[32,8,16,256]{3,2,1,0:T(8,128)(2,1)}, bf16[32,8,16,256]{3,2,1,0:T(8,128)(2,1)}, f32[32,32]{1,0:T(8,128)}, f32[32,32]{1,0:T(8,128)}) custom-call(f32[32,128]{1,0:T(8,128)S(1)} %get-tuple-element.17.products, f32[32,16,128]{2,1,0:T(8,128)S(1)} %all_to_all.5.gathered, bf16[8,2,2,256,256]{4,3,2,1,0:T(8,128)(2,1)S(1)} %get-tuple-element.20.fields, ...), custom_call_target="tpu_custom_call" | custom-call | tf_op jit(solution)/shard_map/finish/pallas_call | solution.py:613
Async XLA Ops:
  3.7 11.1 %collective-permute-start = (bf16[32,16,256]{2,1,0:T(8,128)(2,1)S(1)}, bf16[32,16,256]{2,1,0:T(8,128)(2,1)S(1)}, u32[]{:S(2)}, u32[]{:S(2)}) collective-permute-start(bf16[32,16,256]{2,1,0:T(8,128)(2,1)S(1)} %get-tuple-element.22), channel_id=1, source_target_pairs={{0,4},{8,12},{16,20},{24,28},{4,0},{12,8},{20,16},{28,24},{1,5},{9... | collective-permute-start | bytes 786440 | tf_op jit(solution)/shard_map/ppermute | solution.py:525
  4.2 10.6 %collective-permute-start.1 = (bf16[32,16,256]{2,1,0:T(8,128)(2,1)S(1)}, bf16[32,16,256]{2,1,0:T(8,128)(2,1)S(1)}, u32[]{:S(2)}, u32[]{:S(2)}) collective-permute-start(bf16[32,16,256]{2,1,0:T(8,128)(2,1)S(1)} %get-tuple-element.23), channel_id=1, source_target_pairs={{4,8},{12,16},{20,24},{8,4},{16,12},{24,20},{5,9},{13,17},{21,25},... | collective-permute-start | bytes 786440 | tf_op jit(solution)/shard_map/ppermute | solution.py:525
  4.9 9.9 %collective-permute-start.2 = (bf16[256,256]{1,0:T(8,128)(2,1)S(1)}, bf16[256,256]{1,0:T(8,128)(2,1)S(1)}, u32[]{:S(2)}, u32[]{:S(2)}) collective-permute-start(bf16[256,256]{1,0:T(8,128)(2,1)S(1)} %get-tuple-element.24), channel_id=1, source_target_pairs={{0,1},{2,3},{1,0},{3,2},{4,5},{6,7},{5,4},{7,6},{8,9},{10,11},{9,8... | collective-permute-start | bytes 393224 | tf_op jit(solution)/shard_map/ppermute | solution.py:525
  7.5 7.3 %collective-permute-start.3 = (bf16[256,256]{1,0:T(8,128)(2,1)S(1)}, bf16[256,256]{1,0:T(8,128)(2,1)S(1)}, u32[]{:S(2)}, u32[]{:S(2)}) collective-permute-start(bf16[256,256]{1,0:T(8,128)(2,1)S(1)} %get-tuple-element.25), channel_id=1, source_target_pairs={{1,2},{2,1},{5,6},{6,5},{9,10},{10,9},{13,14},{14,13},{17,18},{18,... | collective-permute-start | bytes 393224 | tf_op jit(solution)/shard_map/ppermute | solution.py:525

commit v7 on v6

--- a/solution.py
+++ b/solution.py
@@ -264,7 +264,7 @@
 
     second_upper, second = cholesky_inverse(gram + SECOND_SHIFT * on, newton)
     upper = state[0]
-    inputs = mm(second, inputs)
+    inputs = mm_three(second, inputs)
     products[...] = jnp.concatenate(
         [mm(second_upper, upper), second, upper, inputs, jnp.zeros((WINDOW, 16), f32)], axis=1
     )
@@ -348,7 +348,7 @@
     image_gram = reduce_rows(image_a[...]) * weight
     image_gram = 0.5 * (image_gram + image_gram.T)
     second = products[:, WINDOW : 2 * WINDOW]
-    image_gram = mm(mm(second, image_gram), second, NT)
+    image_gram = mm_three(mm_three(second, image_gram), second, NT)
     lower = jnp.where(iota(image_gram.shape, 0) > iota(image_gram.shape, 1), image_gram, 0.0)
     inputs = products[:, 3 * WINDOW : 3 * WINDOW + 16]
     rest = [pack(inputs), pack(diagonal_of(image_gram)), jnp.zeros((SUB, 60), f32)]

time: 54.5 us -> 54.4 us (level)
  no operation moved by 1% of the time
where the time goes in v7:
time: 54.4 us; the launch traced here: 54.2 us
  Pallas kernels  29.5 us (54%)
  blocking collectives  18.5 us (34%)
  starting transfers between devices  4.5 us (8%)
  between operations  1.53 us (3%)
    all_to_all x1, blocking collectives, local(): gathered = lax.all_to_all(payload, ('gx', 'gy'), 0, 0)  18.5 us
    pallas_call x1, Pallas kernels, local(): pl.pallas_call(finish_kernel, out_shape=(shape(window_shape, bf16), shape...  15.6 us
    pallas_call x1, Pallas kernels, local(): pl.pallas_call(functools.partial(transform_kernel, weight), out_shape=(sh...  6.59 us
    pallas_call x1, Pallas kernels, local(): pl.pallas_call(functools.partial(project_kernel, weight), out_shape=(shap...  5.11 us
    ppermute x4, starting transfers between devices, exchange(): return lax.ppermute(face, axis, pairs + [(b, a) for a, b in pairs])  4.5 us
    pallas_call x1, Pallas kernels, local(): pl.pallas_call(face_kernel, out_shape=(shape(rows_shape, bf16), x_face, x...  2.29 us
  transfers between devices with their start and end apart: 4, of which 0 were waited for; matrix products, arithmetic and copies ran while one was open for 0% of the time, Pallas kernels for 12%

profile of v7, /device:TPU:0, one launch (start us, length us, event | category | flops | bytes accessed | tf_op | source)
XLA Modules:
  0.0 54.2 jit_solution(12111798504516842857)
XLA Ops:
  1.3 0.1 pad_add_fusion.scalars
  1.4 2.3 %faces.1 = (bf16[8,2,256,256]{3,2,1,0:T(8,128)(2,1)S(1)}, bf16[32,16,256]{2,1,0:T(8,128)(2,1)S(1)}, bf16[32,16,256]{2,1,0:T(8,128)(2,1)S(1)}, bf16[256,256]{1,0:T(8,128)(2,1)S(1)}, bf16[256,256]{1,0:T(8,128)(2,1)S(1)}) custom-call(s32[3]{0:T(128)S(1)} %pad_add_fusion.scalars, bf16[64,8,16,256]{3,2,1,0:T(8,128)(2,1)} %factor.1), custom_call_target="tpu_custom_call" | custom-call | tf_op jit(solution)/shard_map/faces/pallas_call | solution.py:552
  3.7 0.5 collective-permute-start
  4.2 0.7 %collective-permute-start.1 = (bf16[32,16,256]{2,1,0:T(8,128)(2,1)S(1)}, bf16[32,16,256]{2,1,0:T(8,128)(2,1)S(1)}, u32[]{:S(2)}, u32[]{:S(2)}) collective-permute-start(bf16[32,16,256]{2,1,0:T(8,128)(2,1)S(1)} %get-tuple-element.23), channel_id=1, source_target_pairs={{4,8},{12,16},{20,24},{8,4},{16,12},{24,20},{5,9},{13,17},{21,25},... | collective-permute-start | bytes 786440 | tf_op jit(solution)/shard_map/ppermute | solution.py:525
  4.9 2.7 %collective-permute-start.2 = (bf16[256,256]{1,0:T(8,128)(2,1)S(1)}, bf16[256,256]{1,0:T(8,128)(2,1)S(1)}, u32[]{:S(2)}, u32[]{:S(2)}) collective-permute-start(bf16[256,256]{1,0:T(8,128)(2,1)S(1)} %get-tuple-element.24), channel_id=1, source_target_pairs={{0,1},{2,3},{1,0},{3,2},{4,5},{6,7},{5,4},{7,6},{8,9},{10,11},{9,8... | collective-permute-start | bytes 393224 | tf_op jit(solution)/shard_map/ppermute | solution.py:525
  7.5 0.7 %collective-permute-start.3 = (bf16[256,256]{1,0:T(8,128)(2,1)S(1)}, bf16[256,256]{1,0:T(8,128)(2,1)S(1)}, u32[]{:S(2)}, u32[]{:S(2)}) collective-permute-start(bf16[256,256]{1,0:T(8,128)(2,1)S(1)} %get-tuple-element.25), channel_id=1, source_target_pairs={{1,2},{2,1},{5,6},{6,5},{9,10},{10,9},{13,14},{14,13},{17,18},{18,... | collective-permute-start | bytes 393224 | tf_op jit(solution)/shard_map/ppermute | solution.py:525
  8.2 6.6 %transform.1 = (bf16[2,256,256]{2,1,0:T(8,128)(2,1)S(1)}, f32[8,2,256,256]{3,2,1,0:T(8,128)S(1)}, bf16[8,2,2,256,256]{4,3,2,1,0:T(8,128)(2,1)S(1)}, f32[32,128]{1,0:T(8,128)S(1)}, f32[8,16,256]{2,1,0:T(8,128)S(1)}) custom-call(bf16[8,2,256,256]{3,2,1,0:T(8,128)(2,1)S(1)} %get-tuple-element.16.blocks, bf16[8,8,16,256]{3,2,1,0:T(8,128)(2,1)} %actuators_hbm.1, ...), custom_call_target="tpu_custom_call" | custom-call | flops 2000000000 | bytes 8388608 | tf_op jit(solution)/shard_map/transform/pallas_call | solution.py:574
  14.8 0.0 collective-permute-done.2.y_even
  14.8 0.0 collective-permute-done.3.y_odd
  14.8 0.0 collective-permute-done.x_even
  14.8 0.0 collective-permute-done.1.x_odd
  14.8 5.1 %project.1 = (f32[32,16,128]{2,1,0:T(8,128)S(1)}, bf16[8,2,2,256,256]{4,3,2,1,0:T(8,128)(2,1)S(1)}) custom-call(s32[3]{0:T(128)S(1)} %pad_add_fusion.scalars, bf16[2,256,256]{2,1,0:T(8,128)(2,1)S(1)} %get-tuple-element.18.frame, f32[8,2,256,256]{3,2,1,0:T(8,128)S(1)} %get-tuple-element.19.rows_all, ...), custom_call_target="tpu_custom_call" | custom-call | tf_op jit(solution)/shard_map/project/pallas_call | solution.py:597
  19.9 18.5 %all_to_all.5.gathered = f32[32,16,128]{2,1,0:T(8,128)S(1)} all-to-all(f32[32,16,128]{2,1,0:T(8,128)S(1)} %get-tuple-element.26), channel_id=1, replica_groups=mesh['gx'=8,'gy'=4] {'gx','gy'}, dimensions={0} | all-to-all | bytes 524288 | tf_op jit(solution)/shard_map/all_to_all | solution.py:612
  38.4 15.6 %finish.1 = (bf16[32,8,16,256]{3,2,1,0:T(8,128)(2,1)}, bf16[32,8,16,256]{3,2,1,0:T(8,128)(2,1)}, f32[32,32]{1,0:T(8,128)}, f32[32,32]{1,0:T(8,128)}) custom-call(f32[32,128]{1,0:T(8,128)S(1)} %get-tuple-element.17.products, f32[32,16,128]{2,1,0:T(8,128)S(1)} %all_to_all.5.gathered, bf16[8,2,2,256,256]{4,3,2,1,0:T(8,128)(2,1)S(1)} %get-tuple-element.20.fields, ...), custom_call_target="tpu_custom_call" | custom-call | tf_op jit(solution)/shard_map/finish/pallas_call | solution.py:613
Async XLA Ops:
  3.7 11.1 %collective-permute-start = (bf16[32,16,256]{2,1,0:T(8,128)(2,1)S(1)}, bf16[32,16,256]{2,1,0:T(8,128)(2,1)S(1)}, u32[]{:S(2)}, u32[]{:S(2)}) collective-permute-start(bf16[32,16,256]{2,1,0:T(8,128)(2,1)S(1)} %get-tuple-element.22), channel_id=1, source_target_pairs={{0,4},{8,12},{16,20},{24,28},{4,0},{12,8},{20,16},{28,24},{1,5},{9... | collective-permute-start | bytes 786440 | tf_op jit(solution)/shard_map/ppermute | solution.py:525
  4.2 10.6 %collective-permute-start.1 = (bf16[32,16,256]{2,1,0:T(8,128)(2,1)S(1)}, bf16[32,16,256]{2,1,0:T(8,128)(2,1)S(1)}, u32[]{:S(2)}, u32[]{:S(2)}) collective-permute-start(bf16[32,16,256]{2,1,0:T(8,128)(2,1)S(1)} %get-tuple-element.23), channel_id=1, source_target_pairs={{4,8},{12,16},{20,24},{8,4},{16,12},{24,20},{5,9},{13,17},{21,25},... | collective-permute-start | bytes 786440 | tf_op jit(solution)/shard_map/ppermute | solution.py:525
  4.9 9.9 %collective-permute-start.2 = (bf16[256,256]{1,0:T(8,128)(2,1)S(1)}, bf16[256,256]{1,0:T(8,128)(2,1)S(1)}, u32[]{:S(2)}, u32[]{:S(2)}) collective-permute-start(bf16[256,256]{1,0:T(8,128)(2,1)S(1)} %get-tuple-element.24), channel_id=1, source_target_pairs={{0,1},{2,3},{1,0},{3,2},{4,5},{6,7},{5,4},{7,6},{8,9},{10,11},{9,8... | collective-permute-start | bytes 393224 | tf_op jit(solution)/shard_map/ppermute | solution.py:525
  7.5 7.3 %collective-permute-start.3 = (bf16[256,256]{1,0:T(8,128)(2,1)S(1)}, bf16[256,256]{1,0:T(8,128)(2,1)S(1)}, u32[]{:S(2)}, u32[]{:S(2)}) collective-permute-start(bf16[256,256]{1,0:T(8,128)(2,1)S(1)} %get-tuple-element.25), channel_id=1, source_target_pairs={{1,2},{2,1},{5,6},{6,5},{9,10},{10,9},{13,14},{14,13},{17,18},{18,... | collective-permute-start | bytes 393224 | tf_op jit(solution)/shard_map/ppermute | solution.py:525
